TPU v7x, 128 devices: a whole 4x4x4 slice. The times are simulated.
128 devices in a mesh: blk: 32 (over x, z, core), grp: 4 (over y).
Axes of the slice: x: 4, y: 4, z: 4, core: 2. Of those that a mesh axis runs over, the one named last changes fastest.
Arguments:
- tokens: bfloat16 [2048, 8192], P(('blk', 'grp')), may hold values from -6 to 6
- cotangent: bfloat16 [2048, 8192], P(('blk', 'grp')), may hold values from -6 to 6
- gate_weight: bfloat16 [8192, 4096], P(None, 'blk'), may hold values from -0.0625 to 0.0625
- up_weight: bfloat16 [8192, 4096], P(None, 'blk'), may hold values from -0.0625 to 0.0625
- down_weight: bfloat16 [4096, 8192], P('blk'), may hold values from -0.09375 to 0.09375
- a_gate: bfloat16 [256, 16, 8192], P('blk'), may hold values from -0.0625 to 0.0625
- a_up: bfloat16 [256, 16, 8192], P('blk'), may hold values from -0.0625 to 0.0625
- down_output_factors: bfloat16 [256, 16, 8192], P('blk'), may hold values from -0.375 to 0.375
- b_gate: bfloat16 [256, 16, 4096], P(None, None, 'blk'), may hold values from -0.375 to 0.375
- b_up: bfloat16 [256, 16, 4096], P(None, None, 'blk'), may hold values from -0.375 to 0.375
- a_down: bfloat16 [256, 16, 4096], P(None, None, 'blk'), may hold values from -0.09375 to 0.09375
- tenant_of_row: int32 [2048], replicated, may hold values from 0 to 255, as said below
- adapter_slot: int32 [256], replicated, may hold values from 0 to 255, as said below
Outputs:
- mixed: bfloat16 [2048, 8192], P(('blk', 'grp'))
- input_grad: bfloat16 [2048, 8192], P(('blk', 'grp'))
- grad_a_gate: float32 [256, 16, 8192], P(('blk', 'grp'))
- grad_a_up: float32 [256, 16, 8192], P(('blk', 'grp'))
- grad_b_down: float32 [256, 16, 8192], P(('blk', 'grp'))
- grad_b_gate: float32 [256, 16, 4096], P('grp', None, 'blk')
- grad_b_up: float32 [256, 16, 4096], P('grp', None, 'blk')
- grad_a_down: float32 [256, 16, 4096], P('grp', None, 'blk')
Inputs may be any that keep to these rules, and one draw needn't show every extreme that they name: `tenant_of_row`: among the rows held by the devices of one index of grp, for each index b of blk at most 32 rows have tenants whose adapter slot s has s // 8 == b, and for some b exactly 32 do. A permutation: tenant t's factors in a_gate, a_up and down_output_factors, and its gradients of them, stand at index adapter_slot[t].
All inputs are finite; a program needn't handle non-finite values.
Results may differ from a plain program's by a relative error of at most 0.02.
Values may be sent and summed in bfloat16 or wider, within the bound.
No kernel may reach another device: no remote copies, remote signals or barrier semaphores. Data moves between devices by JAX's collectives and lax.ppermute only.
A program may use at most 192 MiB of HBM per device.

v0:
```python
import jax
import jax.numpy as jnp
from jax import lax
from jax.experimental import pallas as pl
from jax.experimental.pallas import tpu as pltpu
from jax.sharding import Mesh
from jax.sharding import PartitionSpec as P

RING = 4
CORES = 2
BLK = ("x", "z", "c")
UP = [(i, (i + 1) % RING) for i in range(RING)]
DOWN = [(i, (i - 1) % RING) for i in range(RING)]
SWAP = [(0, 1), (1, 0)]
RANK = 16
LANES = 128
BF = jnp.bfloat16
F32 = jnp.float32


def params(mib):
    return pltpu.CompilerParams(vmem_limit_bytes=mib << 20)


def dot(a, b):
    return jnp.dot(a, b, preferred_element_type=F32)


def dot_nt(a, b):
    return lax.dot_general(a, b, (((1,), (1,)), ((), ())), preferred_element_type=F32)


def iota(shape, dim):
    return lax.broadcasted_iota(jnp.int32, shape, dim)


def folding(rows, first):
    return ((iota((rows, LANES), 0) & 15) + first == iota((rows, LANES), 1)).astype(BF)


def tiling(first, cols):
    return (iota((LANES, cols), 0) == (iota((LANES, cols), 1) & 15) + first).astype(BF)


def project_kernel(
    rel, choose, x, dy, gate_w, up_w, down_w, a_g, a_u, out_f, pre, coef, own, acc_x, acc_dy
):
    j = pl.program_id(0)

    @pl.when(j == 0)
    def _():
        acc_x[...] = jnp.zeros_like(acc_x)
        acc_dy[...] = jnp.zeros_like(acc_dy)

    xv, dv = x[...], dy[...]
    acc_x[:, : 2 * LANES] += dot(xv, jnp.concatenate([gate_w[...], up_w[...]], axis=1))
    acc_x[:, 2 * LANES :] += dot_nt(xv, jnp.concatenate([a_g[...], a_u[...]], axis=0))
    acc_dy[...] += dot_nt(dv, jnp.concatenate([down_w[...], out_f[...]], axis=0))
    cap = choose.shape[0]
    own[:cap, :] = dot(choose[...], xv).astype(BF)
    own[cap:, :] = dot(choose[...], dv).astype(BF)

    @pl.when(j == pl.num_programs(0) - 1)
    def _():
        pre[:, : 2 * LANES] = acc_x[:, : 2 * LANES]
        pre[:, 2 * LANES :] = acc_dy[:, :LANES]
        rows = xv.shape[0]
        mine = rel[...] == (iota((rows, LANES), 1) >> 4)
        zero = jnp.zeros((rows, LANES), F32)
        z_g = jnp.where(mine, acc_x[:, 2 * LANES : 3 * LANES], zero).astype(BF)
        z_u = jnp.where(mine, acc_x[:, 3 * LANES :], zero).astype(BF)
        z_q = jnp.where(mine, 2.0 * acc_dy[:, LANES:], zero).astype(BF)
        packed = (
            dot(z_g, folding(LANES, 0))
            + dot(z_u, folding(LANES, RANK))
            + dot(z_q, folding(LANES, 2 * RANK))
        )
        coef[...] = dot(choose[...], packed.astype(BF)).astype(BF)


def project(rel, choose, both, gate_w, up_w, down_w, a_g, a_u, out_f):
    rows, d = both.shape[0], both.shape[1] // 2
    cap = choose.shape[0]
    width = 1024
    steps = d // width
    tall = pl.BlockSpec((width, LANES), lambda j: (j, 0))
    wide = pl.BlockSpec((LANES, width), lambda j: (0, j))
    return pl.pallas_call(
        project_kernel,
        grid=(steps,),
        in_specs=[
            pl.BlockSpec((rows, 1), lambda j: (0, 0)),
            pl.BlockSpec((cap, rows), lambda j: (0, 0)),
            pl.BlockSpec((rows, width), lambda j: (0, j)),
            pl.BlockSpec((rows, width), lambda j: (0, j + steps)),
            tall,
            tall,
            wide,
            wide,
            wide,
            wide,
        ],
        out_specs=[
            pl.BlockSpec((rows, 3 * LANES), lambda j: (0, 0)),
            pl.BlockSpec((cap, LANES), lambda j: (0, 0)),
            pl.BlockSpec((2 * cap, width), lambda j: (0, j)),
        ],
        out_shape=[
            jax.ShapeDtypeStruct((rows, 3 * LANES), F32),
            jax.ShapeDtypeStruct((cap, LANES), BF),
            jax.ShapeDtypeStruct((2 * cap, d), BF),
        ],
        scratch_shapes=[pltpu.VMEM((rows, 4 * LANES), F32), pltpu.VMEM((rows, 2 * LANES), F32)],
        compiler_params=params(32),
        name="project",
    )(rel, choose, both, both, gate_w, up_w, down_w, a_g, a_u, out_f)


def hidden_kernel(tenant, pos, pos_row, table, pre, b_g, b_u, a_d, values, placed, partial):
    j = pl.program_id(0)
    rows = pre.shape[0]
    wide = 512
    spots = table.shape[0]
    here = (pos[...] == iota((rows, spots), 1)).astype(BF)
    coefs = dot(here, table[...]).astype(BF)
    tiles = [dot(coefs, tiling(k * RANK, wide)) for k in range(3)]
    who = tenant[...]
    extra = [jnp.zeros((rows, LANES), F32) for _ in range(3)]
    factors = (b_g, b_u, a_d)
    count = b_g.shape[0] // wide
    lane_tenant = iota((rows, wide), 1) >> 4
    for k in range(count):
        mine = (who - k * (wide // RANK)) == lane_tenant
        for m in range(3):
            e = jnp.where(mine, tiles[m], 0.0).astype(BF)
            extra[m] += dot(e, factors[m][k * wide : (k + 1) * wide, :])
    gate = pre[:, :LANES] + 2.0 * extra[0]
    up = pre[:, LANES : 2 * LANES] + 2.0 * extra[1]
    grad = pre[:, 2 * LANES :] + extra[2]
    sig = 1.0 / (1.0 + jnp.exp(-gate))
    act = gate * sig
    slope = sig * (1.0 + gate * (1.0 - sig))
    hidden = (act * up).astype(BF)
    grad_gate = (grad * up * slope).astype(BF)
    grad_up = (grad * act).astype(BF)
    values[:, :LANES] = hidden
    values[:, LANES : 2 * LANES] = grad_gate
    values[:, 2 * LANES : 3 * LANES] = grad_up
    values[:, 3 * LANES :] = coefs
    low = jnp.zeros((rows, LANES), F32)
    for left, right, first, scale in (
        (hidden, a_d, 0, 1.0),
        (grad_gate, b_g, RANK, 2.0),
        (grad_up, b_u, 2 * RANK, 2.0),
    ):
        total = jnp.zeros((rows, wide), F32)
        for k in range(count):
            mine = (who - k * (wide // RANK)) == lane_tenant
            z = dot_nt(left, right[k * wide : (k + 1) * wide, :])
            total = jnp.where(mine, z, total)
        low += dot((scale * total).astype(BF), folding(wide, first))
    partial[pl.ds(pl.multiple_of(j * rows, rows), rows), :] = low.astype(BF)

    @pl.when(j == pl.num_programs(0) - 1)
    def _():
        every = partial.shape[0]
        put = (pos_row[...] == iota((spots, every), 0)).astype(BF)
        placed[...] = dot(put, partial[...]).astype(BF)


def hidden_stage(tenant, pos, pos_row, table, pre, b_g, b_u, a_d):
    rows = pre.shape[0]
    part = 128
    whole = lambda a: pl.BlockSpec(a.shape, lambda j: (0, 0))
    spots = table.shape[0]
    return pl.pallas_call(
        hidden_kernel,
        grid=(rows // part,),
        in_specs=[
            pl.BlockSpec((part, 1), lambda j: (j, 0)),
            pl.BlockSpec((part, 1), lambda j: (j, 0)),
            whole(pos_row),
            whole(table),
            pl.BlockSpec((part, 3 * LANES), lambda j: (j, 0)),
            whole(b_g),
            whole(b_u),
            whole(a_d),
        ],
        out_specs=[
            pl.BlockSpec((part, 4 * LANES), lambda j: (j, 0)),
            pl.BlockSpec((spots, LANES), lambda j: (0, 0)),
        ],
        out_shape=[
            jax.ShapeDtypeStruct((rows, 4 * LANES), BF),
            jax.ShapeDtypeStruct((spots, LANES), BF),
        ],
        scratch_shapes=[pltpu.VMEM((rows, LANES), BF)],
        compiler_params=params(40),
        name="hidden_stage",
    )(tenant, pos, pos_row, table, pre, b_g, b_u, a_d)


def left_kernel(rel, choose_t, low, order_m, order_i, values, left):
    rows = rel.shape[0]
    mine = rel[...] == (iota((rows, LANES), 1) >> 4)
    back = dot(choose_t[...], low[...]).astype(BF)
    spread = lambda first, scale: jnp.where(
        mine, scale * dot(back, tiling(first, LANES)), 0.0
    ).astype(BF)
    for_mixed = jnp.concatenate([values[:, :LANES], spread(0, 2.0)], axis=1)
    for_input = jnp.concatenate(
        [values[:, LANES : 3 * LANES], spread(RANK, 1.0), spread(2 * RANK, 1.0)], axis=1
    )
    at = iota((rows, rows), 1)
    left[:, : 2 * LANES] = dot((order_m[...] == at).astype(BF), for_mixed).astype(BF)
    left[:, 2 * LANES :] = dot((order_i[...] == at).astype(BF), for_input).astype(BF)


def left_stage(rel, choose_t, low, order_m, order_i, values):
    rows = rel.shape[0]
    return pl.pallas_call(
        left_kernel,
        out_shape=jax.ShapeDtypeStruct((rows, 6 * LANES), BF),
        compiler_params=params(40),
        name="left_stage",
    )(rel, choose_t, low, order_m, order_i, values)


def product_kernel(core, left, other, down_w, out_f, gate_w, up_w, a_g, a_u, near, side, *outs):
    del core
    m, i = 2 * LANES, 4 * LANES
    total = dot(left[:, :m], jnp.concatenate([down_w[...], out_f[...]], axis=0))
    total += dot(other[:, :m], near[:m, :])
    mixed = total.astype(BF)
    total = dot_nt(left[:, m:i], jnp.concatenate([gate_w[...], up_w[...]], axis=1))
    total += dot(left[:, i:], jnp.concatenate([a_g[...], a_u[...]], axis=0))
    total += dot_nt(other[:, m:i], side[...])
    total += dot(other[:, i:], near[m:, :])
    back = total.astype(BF)
    n = mixed.shape[0] // 4
    h = n // 2
    for at, value in ((0, mixed), (7, back)):
        for k, (first, count) in enumerate(
            ((0, n), (n, h), (n + h, h), (2 * n, h), (2 * n + h, h), (3 * n, h), (3 * n + h, h))
        ):
            outs[at + k][...] = value[first : first + count, :]


def products(core, left, other, down_w, out_f, gate_w, up_w, a_g, a_u, near, side):
    rows, half = left.shape[0], near.shape[1]
    width = 512
    steps = half // width
    n = rows // 4
    whole = lambda a: pl.BlockSpec(a.shape, lambda j, c: (0, 0))
    wide = pl.BlockSpec((LANES, width), lambda j, c: (0, c[0] * steps + j))
    tall = pl.BlockSpec((width, LANES), lambda j, c: (c[0] * steps + j, 0))
    counts = 2 * [n, n // 2, n // 2, n // 2, n // 2, n // 2, n // 2]
    return pl.pallas_call(
        product_kernel,
        grid_spec=pltpu.PrefetchScalarGridSpec(
            num_scalar_prefetch=1,
            grid=(steps,),
            in_specs=[
                whole(left),
                whole(other),
                wide,
                wide,
                tall,
                tall,
                wide,
                wide,
                pl.BlockSpec((near.shape[0], width), lambda j, c: (0, j)),
                pl.BlockSpec((width, side.shape[1]), lambda j, c: (j, 0)),
            ],
            out_specs=[pl.BlockSpec((k, width), lambda j, c: (0, j)) for k in counts],
        ),
        out_shape=[jax.ShapeDtypeStruct((k, half), BF) for k in counts],
        compiler_params=params(40),
        name="products",
    )(core, left, other, down_w, out_f, gate_w, up_w, a_g, a_u, near, side)


def tenant_kernel(rel_tenant, values, out_bg, out_bu, out_ad):
    groups = rel_tenant.shape[0]
    some = 256
    rows = rel_tenant.shape[1]
    sub = iota((some, rows), 0)
    for out, left, first, scale in (
        (out_bg, 1, 0, 2.0),
        (out_bu, 2, RANK, 2.0),
        (out_ad, 0, 2 * RANK, 1.0),
    ):
        pick = (iota((some, LANES), 1) == (iota((some, LANES), 0) & 15) + first).astype(BF)
        sums = [jnp.zeros((some, LANES), F32) for _ in range(out.shape[0] // some)]
        for g in range(groups):
            tile = dot_nt(pick, values[g, :rows, 3 * LANES :])
            rhs = values[g, :rows, left * LANES : (left + 1) * LANES]
            who = rel_tenant[g : g + 1, :]
            for k in range(len(sums)):
                mine = (who - k * (some // RANK)) == (sub >> 4)
                sums[k] += dot(jnp.where(mine, tile, 0.0).astype(BF), rhs)
        for k, total in enumerate(sums):
            out[k * some : (k + 1) * some, :] = scale * total


def tenant_gradients(rel_tenant, values, tenants):
    shape = jax.ShapeDtypeStruct((tenants * RANK, LANES), F32)
    return pl.pallas_call(
        tenant_kernel,
        out_shape=[shape] * 3,
        compiler_params=params(40),
        name="tenant_gradients",
    )(rel_tenant, values)


def slot_kernel(weights, own, out_g, out_u, out_d):
    groups, cap = own.shape[0], own.shape[1] // 2
    x = jnp.concatenate([own[g, :cap, :] for g in range(groups)], axis=0)
    dy = jnp.concatenate([own[g, cap:, :] for g in range(groups)], axis=0)
    n = out_g.shape[0]
    both = dot(weights[: 2 * n, :], x)
    out_g[...] = both[:n, :]
    out_u[...] = both[n:, :]
    out_d[...] = dot(weights[2 * n :, :], dy)


def slot_gradients(weights, own):
    groups, rows, d = own.shape
    n = weights.shape[0] // 3
    width = 1024
    spec = pl.BlockSpec((n, width), lambda j: (0, j))
    return pl.pallas_call(
        slot_kernel,
        grid=(d // width,),
        in_specs=[
            pl.BlockSpec(weights.shape, lambda j: (0, 0)),
            pl.BlockSpec((groups, rows, width), lambda j: (0, 0, j)),
        ],
        out_specs=[spec] * 3,
        out_shape=[jax.ShapeDtypeStruct((n, d), F32)] * 3,
        compiler_params=params(32),
        name="slot_gradients",
    )(weights, own)


def add(*terms):
    total = terms[0].astype(F32)
    for t in terms[1:]:
        total = total + t.astype(F32)
    return total.astype(BF)


def first_step(a, b, axes, *beside):
    sent = []
    for p, axis in ((a, axes[0]), (b, axes[1])):
        sent += [lax.ppermute(p[3], axis, UP), lax.ppermute(p[4], axis, DOWN)]
    done = lax.optimization_barrier((*sent, *beside))
    return done[:4], done[4:]


def second_start(a, b, axes, sent):
    moved = []
    for k, (p, axis) in enumerate(((a, axes[0]), (b, axes[1]))):
        right = jnp.concatenate([add(p[1], sent[2 * k]), p[2]], axis=0)
        left = jnp.concatenate([p[5], add(p[6], sent[2 * k + 1])], axis=0)
        moved += [lax.ppermute(right, axis, UP), lax.ppermute(left, axis, DOWN)]
    return moved


def second_end(a, b, moved, *beside):
    done = lax.optimization_barrier((*moved, *beside))
    moved, beside = done[:4], done[4:]
    return add(a[0], moved[0], moved[1]), add(b[0], moved[2], moved[3]), beside


def ring_near(v, axis):
    return lax.ppermute(v, axis, UP), lax.ppermute(v, axis, DOWN)


def ring_far(left, right, axis):
    h = left.shape[0] // 2
    return lax.ppermute(left[:h], axis, UP), lax.ppermute(right[h:], axis, DOWN)


def ring_join(v, near, far):
    return jnp.stack([v, *near, jnp.concatenate(far, axis=0)], axis=0)


def sevenths(v):
    n = v.shape[0] // 4
    h = n // 2
    cut = lambda first, count: v[first : first + count]
    return (
        cut(0, n),
        cut(n, h),
        cut(n + h, h),
        cut(2 * n, h),
        cut(2 * n + h, h),
        cut(3 * n, h),
        cut(3 * n + h, h),
    )


def local(
    tokens,
    cotangent,
    gate_weight,
    up_weight,
    down_weight,
    a_gate,
    a_up,
    down_output_factors,
    b_gate,
    b_up,
    a_down,
    tenant_of_row,
    adapter_slot,
):
    own_rows, d = tokens.shape
    half = d // CORES
    blk_count = lax.axis_size(BLK)
    grp_count = lax.axis_size("y")
    x_at, z_at, c_at, grp = (lax.axis_index(k) for k in ("x", "z", "c", "y"))
    blk = (x_at * RING + z_at) * CORES + c_at
    per_owner = a_gate.shape[0]
    tenant_count = b_gate.shape[0]
    cap = 2 * own_rows
    group_rows = own_rows * blk_count

    a_g = a_gate.reshape(per_owner * RANK, d)
    a_u = a_up.reshape(per_owner * RANK, d)
    out_f = down_output_factors.reshape(per_owner * RANK, d)
    b_g = b_gate.reshape(tenant_count * RANK, -1)
    b_u = b_up.reshape(tenant_count * RANK, -1)
    a_d = a_down.reshape(tenant_count * RANK, -1)

    all_tenants = jnp.transpose(tenant_of_row.reshape(blk_count, grp_count, own_rows), (1, 0, 2))
    all_tenants = all_tenants.reshape(grp_count, group_rows)
    hot = all_tenants[:, :, None] == jnp.arange(tenant_count, dtype=jnp.int32)
    all_slots = jnp.sum(jnp.where(hot, adapter_slot, 0), axis=2)
    all_owners = all_slots // per_owner
    at = jnp.arange(group_rows, dtype=jnp.int32)
    ahead = (all_owners[:, :, None] == all_owners[:, None, :]) & (at[:, None] > at[None, :])
    all_within = jnp.sum(ahead.astype(jnp.int32), axis=2)
    mine = all_owners == blk
    all_choose = mine[:, None, :] & (
        all_within[:, None, :] == jnp.arange(cap, dtype=jnp.int32)[None, :, None]
    )
    own_slot = jnp.sum(jnp.where(all_choose, (all_slots - per_owner * blk)[:, None, :] + 1, 0), 2) - 1
    here = lambda v: lax.dynamic_index_in_dim(v, grp, 0, keepdims=False)
    tenants, slots = here(all_tenants), here(all_slots)
    position = here(all_owners) * cap + here(all_within)
    choose = here(all_choose).astype(BF)
    rel = slots - per_owner * blk

    far = (1 - c_at) * half
    cut_wide = lambda v: lax.dynamic_slice_in_dim(v, far, half, 1)
    cut_tall = lambda v: lax.dynamic_slice_in_dim(v, far, half, 0)
    near = jnp.concatenate([cut_wide(v) for v in (down_weight, out_f, a_g, a_u)], axis=0)
    side = jnp.concatenate([cut_tall(gate_weight), cut_tall(up_weight)], axis=1)
    near = lax.ppermute(near, "c", SWAP)
    side = lax.ppermute(side, "c", SWAP)

    j = jnp.arange(group_rows, dtype=jnp.int32)
    inner = j % (CORES * own_rows)
    first, second = j // (group_rows // RING), (j // (CORES * own_rows)) % RING
    place = lambda dx, dz: (
        ((x_at + dx) % RING * RING + (z_at + dz) % RING) * CORES * own_rows + inner
    )[:, None]
    order_m, order_i = place(first, second), place(second, first)

    both = jnp.concatenate([tokens, cotangent], axis=1)
    both = lax.all_gather(both, BLK, axis=0, tiled=True)
    rel = rel[:, None]
    pre, coef, own = project(
        rel, choose, both, gate_weight, up_weight, down_weight, a_g, a_u, out_f
    )
    own_near = ring_near(own, "y")
    copies = jnp.broadcast_to(coef[:, : 3 * RANK], (blk_count, cap, 3 * RANK))
    table = lax.all_to_all(copies, BLK, split_axis=0, concat_axis=0, tiled=True)
    table = jnp.pad(table.reshape(blk_count * cap, 3 * RANK), ((0, 0), (0, LANES - 3 * RANK)))
    values, placed = hidden_stage(
        tenants[:, None], position[:, None], position[None, :], table, pre, b_g, b_u, a_d
    )
    placed, *own_near = lax.optimization_barrier((placed, *own_near))
    own_far = ring_far(*own_near, "y")
    terms = placed[:, : 3 * RANK].reshape(blk_count, cap, 3 * RANK)
    terms = lax.all_to_all(terms, BLK, split_axis=0, concat_axis=0, tiled=True)
    low = jnp.sum(terms.astype(F32), axis=0).astype(BF)
    low = jnp.pad(low, ((0, cap), (0, LANES - 3 * RANK)))
    left = left_stage(rel, jnp.transpose(choose), low[:cap], order_m, order_i, values)
    other = lax.ppermute(left, "c", SWAP)
    packed = jnp.concatenate([values, low.reshape(-1, 4 * LANES)], axis=0)
    left, other, packed, *own_far = lax.optimization_barrier((left, other, packed, *own_far))
    packed_near = ring_near(packed, "y")
    pieces = products(
        c_at.reshape(1).astype(jnp.int32),
        left,
        other,
        down_weight,
        out_f,
        gate_weight,
        up_weight,
        a_g,
        a_u,
        near,
        side,
    )
    pieces = (pieces[:7], pieces[7:])
    sent, packed_near = first_step(*pieces, ("x", "z"), *packed_near)
    moved = second_start(*pieces, ("x", "z"), sent)
    packed_far = ring_far(*packed_near, "y")

    all_own = ring_join(own, own_near, own_far)
    packed = ring_join(packed, packed_near, packed_far)
    turn = (grp + jnp.array([0, -1, 1, 2], jnp.int32)) % grp_count
    turned = lambda v: jnp.sum(
        jnp.where((turn[:, None] == jnp.arange(grp_count, dtype=jnp.int32))[:, :, None], v[None], 0), 1
    )
    low_all = packed[:, group_rows:, :].astype(F32)
    low_all = low_all.reshape(grp_count, -1, LANES)[:, :cap, : 3 * RANK]
    slots_dev = per_owner // grp_count
    wanted = grp * slots_dev + jnp.arange(slots_dev, dtype=jnp.int32)
    weights = jnp.where(
        (turned(own_slot)[None] == wanted[:, None, None])[:, None],
        jnp.transpose(low_all, (2, 0, 1))[None],
        0.0,
    )
    weights = weights.reshape(slots_dev, 3, RANK, grp_count * cap)
    weights = jnp.transpose(weights, (1, 0, 2, 3)).reshape(3, slots_dev * RANK, grp_count * cap)
    weights = jnp.concatenate([weights[1], weights[2], 2.0 * weights[0]], axis=0).astype(BF)
    by_slot = slot_gradients(weights, all_own)
    tenant_dev = tenant_count // grp_count
    by_tenant = tenant_gradients(turned(all_tenants) - grp * tenant_dev, packed, tenant_dev)

    *sums, grads = second_end(*pieces, moved, *by_slot, *by_tenant)
    pieces = (sevenths(sums[0]), sevenths(sums[1]))
    sent, _ = first_step(*pieces, ("z", "x"))
    moved = second_start(*pieces, ("z", "x"), sent)
    *sums, _ = second_end(*pieces, moved)
    stacked = jnp.stack([v.reshape(CORES, own_rows, half) for v in sums], axis=1)
    keep = lax.dynamic_index_in_dim(stacked, c_at, 0, keepdims=False)
    give = lax.dynamic_index_in_dim(stacked, 1 - c_at, 0, keepdims=False)
    take = lax.ppermute(give, "c", SWAP)
    result = jnp.where(
        c_at == 0,
        jnp.concatenate([keep, take], axis=2),
        jnp.concatenate([take, keep], axis=2),
    )
    return (
        result[0],
        result[1],
        *(v.reshape(slots_dev, RANK, d) for v in grads[:3]),
        *(v.reshape(tenant_dev, RANK, -1) for v in grads[3:]),
    )


def solution(mesh):
    cut = Mesh(mesh.devices.reshape(RING, RING, CORES, mesh.shape["grp"]), ("x", "z", "c", "y"))
    every = (*BLK, "y")
    return jax.shard_map(
        local,
        mesh=cut,
        in_specs=(
            P(every, None),
            P(every, None),
            P(None, BLK),
            P(None, BLK),
            P(BLK, None),
            P(BLK, None, None),
            P(BLK, None, None),
            P(BLK, None, None),
            P(None, None, BLK),
            P(None, None, BLK),
            P(None, None, BLK),
            P(),
            P(),
        ),
        out_specs=(
            P(every, None),
            P(every, None),
            P(every, None, None),
            P(every, None, None),
            P(every, None, None),
            P("y", None, BLK),
            P("y", None, BLK),
            P("y", None, BLK),
        ),
        check_vma=False,
    )
```

profile of v0, /device:TPU:1, one launch (start us, length us, event | category | flops | bytes accessed | tf_op | source)
XLA Modules:
  0.0 290.9 jit_solution(8028440686594691507)
XLA Ops:
  12.1 2.4 pad_maximum_fusion
  22.6 64.6 %all-gather.2.cloned.1.call-done.x.dy = bf16[512,16384]{1,0:T(8,128)(2,1)} async-done(((bf16[16,16384]{1,0:T(8,128)(2,1)}), bf16[512,16384]{1,0:T(8,128)(2,1)}) %all-gather.2.cloned.1.call-update) | async-done | bytes 16777232 | tf_op jit(solution)/shard_map/all_gather | solution.py:473
  95.1 14.2 %project.1 = (f32[512,384]{1,0:T(8,128)S(1)}, bf16[32,128]{1,0:T(8,128)(2,1)S(1)}, bf16[64,8192]{1,0:T(8,128)(2,1)}) custom-call(s32[512,1]{1,0:T(8,128)S(1)} %copy.36.rel, bf16[32,512]{1,0:T(8,128)(2,1)S(1)} %copy.33.choose, bf16[512,16384]{1,0:T(8,128)(2,1)} %all-gather.2.cloned.1.call-done.x.dy, bf16[512,16384]{1,0:T(8,128)(2,1)} %all-gather.2.cloned.1.call-done.x.dy, ...), custom_call_target="tpu_custom_call" | custom-call | tf_op jit(solution)/shard_map/project/pallas_call | solution.py:88
  114.6 5.9 %all-to-all-start = ((bf16[32,2,768]{2,1,0:T(2,128)(2,1)}), bf16[32,2,768]{2,1,0:T(2,128)(2,1)S(1)}, u32[]{:S(2)}, u32[]{:S(2)}) async-start(bf16[32,2,768]{2,1,0:T(2,128)(2,1)} %reshape.510), calls=%async_computation | async-start | bytes 196608 | tf_op jit(solution)/shard_map/all_to_all | solution.py:480
  121.2 6.8 %all-to-all-done = bf16[32,2,768]{2,1,0:T(2,128)(2,1)S(1)} async-done(((bf16[32,2,768]{2,1,0:T(2,128)(2,1)}), bf16[32,2,768]{2,1,0:T(2,128)(2,1)S(1)}, u32[]{:S(2)}, u32[]{:S(2)}) %all-to-all-start) | async-done | bytes 98336 | tf_op jit(solution)/shard_map/all_to_all | solution.py:480
  130.8 10.8 %hidden_stage.1 = (bf16[512,512]{1,0:T(8,128)(2,1)S(1)}, bf16[1024,128]{1,0:T(8,128)(2,1)S(1)}) custom-call(s32[512,1]{1,0:T(8,128)S(1)} %copy.34.tenant, s32[512,1]{1,0:T(8,128)S(1)} %copy.35.pos, s32[1,512]{1,0:T(1,128)S(1)} %get-tuple-element.145.pos_row, bf16[1024,128]{1,0:T(8,128)(2,1)S(1)} %pad.8.table, f32[512,384]{1,0:T(8,128)S(1)} %get-tuple-element.66.pre, ...), custom_call_target="tpu_custom_call" | custom-call | tf_op jit(solution)/shard_map/hidden_stage/pallas_call | solution.py:176
  142.6 3.9 %all-to-all-start.1 = ((bf16[32,2,768]{2,1,0:T(2,128)(2,1)}), bf16[32,2,768]{2,1,0:T(2,128)(2,1)S(1)}, u32[]{:S(2)}, u32[]{:S(2)}) async-start(bf16[32,2,768]{2,1,0:T(2,128)(2,1)} %reshape.512), calls=%async_computation.1 | async-start | bytes 196608 | tf_op jit(solution)/shard_map/all_to_all | solution.py:488
  147.0 7.0 %all-to-all-done.1 = bf16[32,2,768]{2,1,0:T(2,128)(2,1)S(1)} async-done(((bf16[32,2,768]{2,1,0:T(2,128)(2,1)}), bf16[32,2,768]{2,1,0:T(2,128)(2,1)S(1)}, u32[]{:S(2)}, u32[]{:S(2)}) %all-to-all-start.1) | async-done | bytes 98336 | tf_op jit(solution)/shard_map/all_to_all | solution.py:488
  159.7 2.7 collective-permute-start.4
  163.6 9.1 %collective-permute-done.3 = bf16[32,8192]{1,0:T(8,128)(2,1)} collective-permute-done((bf16[32,8192]{1,0:T(8,128)(2,1)}, bf16[32,8192]{1,0:T(8,128)(2,1)}, u32[]{:S(2)}, u32[]{:S(2)}) %collective-permute-start.3) | collective-permute-done | bytes 524320 | tf_op jit(solution)/shard_map/ppermute | solution.py:382
  174.2 2.7 collective-permute-start.12
  178.5 11.6 %products.1 = (bf16[128,4096]{1,0:T(8,128)(2,1)S(1)}, bf16[64,4096]{1,0:T(8,128)(2,1)S(1)}, bf16[64,4096]{1,0:T(8,128)(2,1)S(1)}, bf16[64,4096]{1,0:T(8,128)(2,1...) custom-call(s32[1]{0:T(128)} %bitcast.core, ...), custom_call_target="tpu_custom_call" | custom-call | tf_op jit(solution)/shard_map/products/pallas_call | solution.py:258
  195.1 6.9 %collective-permute-done.10 = bf16[64,4096]{1,0:T(8,128)(2,1)S(1)} collective-permute-done((bf16[64,4096]{1,0:T(8,128)(2,1)S(1)}, bf16[64,4096]{1,0:T(8,128)(2,1)S(1)}, u32[]{:S(2)}, u32[]{:S(2)}) %collective-permute-start.10) | collective-permute-done | bytes 524320 | tf_op jit(solution)/shard_map/ppermute | solution.py:356
  202.3 3.6 %pad_maximum_fusion.1.own = bf16[4,64,8192]{2,1,0:T(8,128)(2,1)} fusion(bf16[1,64,8192]{2,1,0:T(8,128)(2,1)S(1)} %maximum_bitcast_fusion, bf16[1,64,8192]{2,1,0:T(8,128)(2,1)} %bitcast.25, bf16[1,64,8192]{2,1,0:T(8,128)(2,1)} %bitcast.24, bf16[1,64,8192]{2,1,0:T(8,128)(2,1)} %bitcast.23), kind=kLoop, calls=%fused_computation.1 | loop fusion | flops 6291456 | bytes 8388608 | tf_op jit(solution)/shard_map/stack | solution.py:386
  205.9 8.1 %collective-permute-done.9 = bf16[64,4096]{1,0:T(8,128)(2,1)S(1)} collective-permute-done((bf16[64,4096]{1,0:T(8,128)(2,1)S(1)}, bf16[64,4096]{1,0:T(8,128)(2,1)S(1)}, u32[]{:S(2)}, u32[]{:S(2)}) %collective-permute-start.9) | collective-permute-done | bytes 524320 | tf_op jit(solution)/shard_map/ppermute | solution.py:356
  214.2 2.7 collective-permute-start.18
  225.3 5.8 %tenant_gradients.1 = (f32[1024,128]{1,0:T(8,128)}, f32[1024,128]{1,0:T(8,128)}, f32[1024,128]{1,0:T(8,128)}) custom-call(s32[4,512]{1,0:T(4,128)S(1)} %broadcast_subtract_fusion.rel_tenant, bf16[4,528,512]{2,1,0:T(8,128)(2,1)S(1)} %pad_maximum_fusion.2.values), custom_call_target="tpu_custom_call" | custom-call | tf_op jit(solution)/shard_map/tenant_gradients/pallas_call | solution.py:308
  233.3 4.0 %slot_gradients.1 = (f32[32,8192]{1,0:T(8,128)}, f32[32,8192]{1,0:T(8,128)}, f32[32,8192]{1,0:T(8,128)}) custom-call(bf16[96,128]{1,0:T(8,128)(2,1)S(1)} %pad_maximum_fusion.14.weights, bf16[4,64,8192]{2,1,0:T(8,128)(2,1)S(1)} %copy-done), custom_call_target="tpu_custom_call" | custom-call | tf_op jit(solution)/shard_map/slot_gradients/pallas_call | solution.py:332
  239.0 3.1 %collective-permute-done.15 = bf16[128,4096]{1,0:T(8,128)(2,1)} collective-permute-done((bf16[128,4096]{1,0:T(8,128)(2,1)}, bf16[128,4096]{1,0:T(8,128)(2,1)}, u32[]{:S(2)}, u32[]{:S(2)}) %collective-permute-start.15) | collective-permute-done | bytes 1048608 | tf_op jit(solution)/shard_map/ppermute | solution.py:366
  242.4 2.9 %collective-permute-done.13 = bf16[128,4096]{1,0:T(8,128)(2,1)} collective-permute-done((bf16[128,4096]{1,0:T(8,128)(2,1)}, bf16[128,4096]{1,0:T(8,128)(2,1)}, u32[]{:S(2)}, u32[]{:S(2)}) %collective-permute-start.13) | collective-permute-done | bytes 1048608 | tf_op jit(solution)/shard_map/ppermute | solution.py:366
  247.5 2.7 collective-permute-start.22
  259.2 3.0 %collective-permute-start.24 = (bf16[32,4096]{1,0:T(8,128)(2,1)S(1)}, bf16[32,4096]{1,0:T(8,128)(2,1)}, u32[]{:S(2)}, u32[]{:S(2)}) collective-permute-start(bf16[32,4096]{1,0:T(8,128)(2,1)S(1)} %pad_maximum_fusion.11), channel_id=1, source_target_pairs={{0,24},{8,0},{16,8},{24,16},{1,25},{9,1},{17,9},{25,17},{2,26},{10... | collective-permute-start | bytes 786440 | tf_op jit(solution)/shard_map/ppermute | solution.py:366
  264.4 2.5 collective-permute-done.24
  271.1 10.9 %collective-permute-start.27 = (bf16[2,16,4096]{2,1,0:T(8,128)(2,1)S(1)}, bf16[2,16,4096]{2,1,0:T(8,128)(2,1)S(1)}, u32[]{:S(2)}, u32[]{:S(2)}) collective-permute-start(bf16[2,16,4096]{2,1,0:T(8,128)(2,1)S(1)} %get-tuple-element.139), channel_id=1, source_target_pairs={{0,4},{4,0},{1,5},{5,1},{2,6},{6,2},{3,7},{7,3},{8,12},{12,8},{9,1... | collective-permute-start | bytes 786440 | tf_op jit(solution)/shard_map/ppermute | solution.py:544
  (178 shorter events, 78.3 us)
Async XLA Ops:
  7.2 80.0 %all-gather.2.cloned.1.call-start = ((), (), s32[]{:S(2)}) async-start(), calls=%async_computation.2 | async-start | bytes 17301504 | tf_op jit(solution)/shard_map/all_gather | solution.py:473
  14.5 162.4 %collective-permute-start.5 = (bf16[512,4096]{1,0:T(8,128)(2,1)}, bf16[512,4096]{1,0:T(8,128)(2,1)}, u32[]{:S(2)}, u32[]{:S(2)}) collective-permute-start(bf16[512,4096]{1,0:T(8,128)(2,1)} %pad_maximum_fusion), channel_id=1, source_target_pairs={{0,4},{4,0},{1,5},{5,1},{2,6},{6,2},{3,7},{7,3},{8,12},{12,8},{9,1... | collective-permute-start | bytes 12582920 | tf_op jit(solution)/shard_map/ppermute | solution.py:461
  17.9 159.0 %collective-permute-start.6 = (bf16[4096,256]{1,0:T(8,128)(2,1)}, bf16[4096,256]{1,0:T(8,128)(2,1)}, u32[]{:S(2)}, u32[]{:S(2)}) collective-permute-start(bf16[4096,256]{1,0:T(8,128)(2,1)} %pad_maximum_fusion.3), channel_id=1, source_target_pairs={{0,4},{4,0},{1,5},{5,1},{2,6},{6,2},{3,7},{7,3},{8,12},{12,8},{9,1... | collective-permute-start | bytes 6291464 | tf_op jit(solution)/shard_map/ppermute | solution.py:462
  109.3 32.3 %collective-permute-start = (bf16[64,8192]{1,0:T(8,128)(2,1)}, bf16[64,8192]{1,0:T(8,128)(2,1)}, u32[]{:S(2)}, u32[]{:S(2)}) collective-permute-start(bf16[64,8192]{1,0:T(8,128)(2,1)} %get-tuple-element.68), channel_id=1, source_target_pairs={{0,1},{1,2},{2,3},{3,0},{4,5},{5,6},{6,7},{7,4},{8,9},{9,10},{10,1... | collective-permute-start | bytes 3145736 | tf_op jit(solution)/shard_map/ppermute | solution.py:377
  110.5 31.1 %collective-permute-start.1 = (bf16[64,8192]{1,0:T(8,128)(2,1)}, bf16[64,8192]{1,0:T(8,128)(2,1)}, u32[]{:S(2)}, u32[]{:S(2)}) collective-permute-start(bf16[64,8192]{1,0:T(8,128)(2,1)} %get-tuple-element.68), channel_id=1, source_target_pairs={{0,3},{1,0},{2,1},{3,2},{4,7},{5,4},{6,5},{7,6},{8,11},{9,8},{10,9... | collective-permute-start | bytes 3145736 | tf_op jit(solution)/shard_map/ppermute | solution.py:377
  114.6 13.4 %all-to-all-start = ((bf16[32,2,768]{2,1,0:T(2,128)(2,1)}), bf16[32,2,768]{2,1,0:T(2,128)(2,1)S(1)}, u32[]{:S(2)}, u32[]{:S(2)}) async-start(bf16[32,2,768]{2,1,0:T(2,128)(2,1)} %reshape.510), calls=%async_computation | async-start | bytes 196608 | tf_op jit(solution)/shard_map/all_to_all | solution.py:480
  142.6 11.5 %all-to-all-start.1 = ((bf16[32,2,768]{2,1,0:T(2,128)(2,1)}), bf16[32,2,768]{2,1,0:T(2,128)(2,1)S(1)}, u32[]{:S(2)}, u32[]{:S(2)}) async-start(bf16[32,2,768]{2,1,0:T(2,128)(2,1)} %reshape.512), calls=%async_computation.1 | async-start | bytes 196608 | tf_op jit(solution)/shard_map/all_to_all | solution.py:488
  155.4 18.1 %collective-permute-start.2 = (bf16[512,768]{1,0:T(8,128)(2,1)S(1)}, bf16[512,768]{1,0:T(8,128)(2,1)}, u32[]{:S(2)}, u32[]{:S(2)}) collective-permute-start(bf16[512,768]{1,0:T(8,128)(2,1)S(1)} %left_stage.1.left), channel_id=1, source_target_pairs={{0,4},{4,0},{1,5},{5,1},{2,6},{6,2},{3,7},{7,3},{8,12},{12,8},{9,1... | collective-permute-start | bytes 2359304 | tf_op jit(solution)/shard_map/ppermute | solution.py:492
  157.9 14.8 %collective-permute-start.3 = (bf16[32,8192]{1,0:T(8,128)(2,1)}, bf16[32,8192]{1,0:T(8,128)(2,1)}, u32[]{:S(2)}, u32[]{:S(2)}) collective-permute-start(bf16[32,8192]{1,0:T(8,128)(2,1)} %slice.93), channel_id=1, source_target_pairs={{0,1},{1,2},{2,3},{3,0},{4,5},{5,6},{6,7},{7,4},{8,9},{9,10},{10,1... | collective-permute-start | bytes 1572872 | tf_op jit(solution)/shard_map/ppermute | solution.py:382
  159.7 13.8 %collective-permute-start.4 = (bf16[32,8192]{1,0:T(8,128)(2,1)}, bf16[32,8192]{1,0:T(8,128)(2,1)}, u32[]{:S(2)}, u32[]{:S(2)}) collective-permute-start(bf16[32,8192]{1,0:T(8,128)(2,1)} %slice.94), channel_id=1, source_target_pairs={{0,3},{1,0},{2,1},{3,2},{4,7},{5,4},{6,5},{7,6},{8,11},{9,8},{10,9... | collective-permute-start | bytes 1572872 | tf_op jit(solution)/shard_map/ppermute | solution.py:382
  173.5 40.6 %collective-permute-start.11 = (bf16[528,512]{1,0:T(8,128)(2,1)S(1)}, bf16[528,512]{1,0:T(8,128)(2,1)S(1)}, u32[]{:S(2)}, u32[]{:S(2)}) collective-permute-start(bf16[528,512]{1,0:T(8,128)(2,1)S(1)} %pad_maximum_fusion.8), channel_id=1, source_target_pairs={{0,1},{1,2},{2,3},{3,0},{4,5},{5,6},{6,7},{7,4},{8,9},{9,10},{10,1... | collective-permute-start | bytes 1622024 | tf_op jit(solution)/shard_map/ppermute | solution.py:377
  174.2 39.9 %collective-permute-start.12 = (bf16[528,512]{1,0:T(8,128)(2,1)S(1)}, bf16[528,512]{1,0:T(8,128)(2,1)S(1)}, u32[]{:S(2)}, u32[]{:S(2)}) collective-permute-start(bf16[528,512]{1,0:T(8,128)(2,1)S(1)} %pad_maximum_fusion.8), channel_id=1, source_target_pairs={{0,3},{1,0},{2,1},{3,2},{4,7},{5,4},{6,5},{7,6},{8,11},{9,8},{10,9... | collective-permute-start | bytes 1622024 | tf_op jit(solution)/shard_map/ppermute | solution.py:377
  190.2 11.8 %collective-permute-start.10 = (bf16[64,4096]{1,0:T(8,128)(2,1)S(1)}, bf16[64,4096]{1,0:T(8,128)(2,1)S(1)}, u32[]{:S(2)}, u32[]{:S(2)}) collective-permute-start(bf16[64,4096]{1,0:T(8,128)(2,1)S(1)} %get-tuple-element.80), channel_id=1, source_target_pairs={{0,24},{8,0},{16,8},{24,16},{1,25},{9,1},{17,9},{25,17},{2,26},{10... | collective-permute-start | bytes 1572872 | tf_op jit(solution)/shard_map/ppermute | solution.py:356
  191.1 14.8 %collective-permute-start.7 = (bf16[64,4096]{1,0:T(8,128)(2,1)S(1)}, bf16[64,4096]{1,0:T(8,128)(2,1)S(1)}, u32[]{:S(2)}, u32[]{:S(2)}) collective-permute-start(bf16[64,4096]{1,0:T(8,128)(2,1)S(1)} %get-tuple-element.77), channel_id=1, source_target_pairs={{0,32},{32,64},{64,96},{96,0},{1,33},{33,65},{65,97},{97,1},{2,34}... | collective-permute-start | bytes 1572872 | tf_op jit(solution)/shard_map/ppermute | solution.py:356
  191.5 14.5 %collective-permute-start.8 = (bf16[64,4096]{1,0:T(8,128)(2,1)S(1)}, bf16[64,4096]{1,0:T(8,128)(2,1)S(1)}, u32[]{:S(2)}, u32[]{:S(2)}) collective-permute-start(bf16[64,4096]{1,0:T(8,128)(2,1)S(1)} %get-tuple-element.78), channel_id=1, source_target_pairs={{0,96},{32,0},{64,32},{96,64},{1,97},{33,1},{65,33},{97,65},{2,98}... | collective-permute-start | bytes 1572872 | tf_op jit(solution)/shard_map/ppermute | solution.py:356
  202.0 12.1 %collective-permute-start.9 = (bf16[64,4096]{1,0:T(8,128)(2,1)S(1)}, bf16[64,4096]{1,0:T(8,128)(2,1)S(1)}, u32[]{:S(2)}, u32[]{:S(2)}) collective-permute-start(bf16[64,4096]{1,0:T(8,128)(2,1)S(1)} %get-tuple-element.79), channel_id=1, source_target_pairs={{0,8},{8,16},{16,24},{24,0},{1,9},{9,17},{17,25},{25,1},{2,10},{10... | collective-permute-start | bytes 1572872 | tf_op jit(solution)/shard_map/ppermute | solution.py:356
  214.1 9.9 %collective-permute-start.17 = (bf16[264,512]{1,0:T(8,128)(2,1)S(1)}, bf16[264,512]{1,0:T(8,128)(2,1)S(1)}, u32[]{:S(2)}, u32[]{:S(2)}) collective-permute-start(bf16[264,512]{1,0:T(8,128)(2,1)S(1)} %slice.95), channel_id=1, source_target_pairs={{0,1},{1,2},{2,3},{3,0},{4,5},{5,6},{6,7},{7,4},{8,9},{9,10},{10,1... | collective-permute-start | bytes 811016 | tf_op jit(solution)/shard_map/ppermute | solution.py:382
  214.2 10.5 %collective-permute-start.18 = (bf16[264,512]{1,0:T(8,128)(2,1)S(1)}, bf16[264,512]{1,0:T(8,128)(2,1)S(1)}, u32[]{:S(2)}, u32[]{:S(2)}) collective-permute-start(bf16[264,512]{1,0:T(8,128)(2,1)S(1)} %slice.96), channel_id=1, source_target_pairs={{0,3},{1,0},{2,1},{3,2},{4,7},{5,4},{6,5},{7,6},{8,11},{9,8},{10,9... | collective-permute-start | bytes 811016 | tf_op jit(solution)/shard_map/ppermute | solution.py:382
  218.1 20.9 %collective-permute-start.16 = (bf16[128,4096]{1,0:T(8,128)(2,1)}, bf16[128,4096]{1,0:T(8,128)(2,1)}, u32[]{:S(2)}, u32[]{:S(2)}) collective-permute-start(bf16[128,4096]{1,0:T(8,128)(2,1)} %pad_maximum_fusion.7), channel_id=1, source_target_pairs={{0,24},{8,0},{16,8},{24,16},{1,25},{9,1},{17,9},{25,17},{2,26},{10... | collective-permute-start | bytes 3145736 | tf_op jit(solution)/shard_map/ppermute | solution.py:366
  220.3 21.8 %collective-permute-start.15 = (bf16[128,4096]{1,0:T(8,128)(2,1)}, bf16[128,4096]{1,0:T(8,128)(2,1)}, u32[]{:S(2)}, u32[]{:S(2)}) collective-permute-start(bf16[128,4096]{1,0:T(8,128)(2,1)} %pad_maximum_fusion.6), channel_id=1, source_target_pairs={{0,8},{8,16},{16,24},{24,0},{1,9},{9,17},{17,25},{25,1},{2,10},{10... | collective-permute-start | bytes 3145736 | tf_op jit(solution)/shard_map/ppermute | solution.py:366
  222.0 20.4 %collective-permute-start.14 = (bf16[128,4096]{1,0:T(8,128)(2,1)}, bf16[128,4096]{1,0:T(8,128)(2,1)}, u32[]{:S(2)}, u32[]{:S(2)}) collective-permute-start(bf16[128,4096]{1,0:T(8,128)(2,1)} %pad_maximum_fusion.5), channel_id=1, source_target_pairs={{0,96},{32,0},{64,32},{96,64},{1,97},{33,1},{65,33},{97,65},{2,98}... | collective-permute-start | bytes 3145736 | tf_op jit(solution)/shard_map/ppermute | solution.py:366
  224.0 21.3 %collective-permute-start.13 = (bf16[128,4096]{1,0:T(8,128)(2,1)}, bf16[128,4096]{1,0:T(8,128)(2,1)}, u32[]{:S(2)}, u32[]{:S(2)}) collective-permute-start(bf16[128,4096]{1,0:T(8,128)(2,1)} %pad_maximum_fusion.4), channel_id=1, source_target_pairs={{0,32},{32,64},{64,96},{96,0},{1,33},{33,65},{65,97},{97,1},{2,34}... | collective-permute-start | bytes 3145736 | tf_op jit(solution)/shard_map/ppermute | solution.py:366
  259.2 7.7 %collective-permute-start.24 = (bf16[32,4096]{1,0:T(8,128)(2,1)S(1)}, bf16[32,4096]{1,0:T(8,128)(2,1)}, u32[]{:S(2)}, u32[]{:S(2)}) collective-permute-start(bf16[32,4096]{1,0:T(8,128)(2,1)S(1)} %pad_maximum_fusion.11), channel_id=1, source_target_pairs={{0,24},{8,0},{16,8},{24,16},{1,25},{9,1},{17,9},{25,17},{2,26},{10... | collective-permute-start | bytes 786440 | tf_op jit(solution)/shard_map/ppermute | solution.py:366
  271.1 12.0 %collective-permute-start.27 = (bf16[2,16,4096]{2,1,0:T(8,128)(2,1)S(1)}, bf16[2,16,4096]{2,1,0:T(8,128)(2,1)S(1)}, u32[]{:S(2)}, u32[]{:S(2)}) collective-permute-start(bf16[2,16,4096]{2,1,0:T(8,128)(2,1)S(1)} %get-tuple-element.139), channel_id=1, source_target_pairs={{0,4},{4,0},{1,5},{5,1},{2,6},{6,2},{3,7},{7,3},{8,12},{12,8},{9,1... | collective-permute-start | bytes 786440 | tf_op jit(solution)/shard_map/ppermute | solution.py:544
  (31 other events, 205.3 us)
Sparse Core Ops, SparseCore 0:
  10.8 76.2 all-gather.1
where the time goes:
time: 292 us; the launch traced here: 291 us
  waiting for transfers between devices  121 us (41%)
  starting transfers between devices  52.6 us (18%)
  Pallas kernels  47.3 us (16%)
  other arithmetic  28.7 us (10%)
  local copies, waits for them, and re-layouts  26.4 us (9%)
  between operations  14.7 us (5%)
    all_gather x1, waiting for transfers between devices, local(): both = lax.all_gather(both, BLK, axis=0, tiled=True)  64.6 us
    unnamed x53, local copies, waits for them, and re-layouts  17.8 us
    ppermute x8, waiting for transfers between devices, first_step(): sent += [lax.ppermute(p[3], axis, UP), lax.ppermute(p[4], axis, DOWN)]  17.4 us
    ppermute x8, waiting for transfers between devices, second_start(): moved += [lax.ppermute(right, axis, UP), lax.ppermute(left, axis, DOWN)]  14.4 us
    pallas_call x1, Pallas kernels, project(): pl.pallas_call(project_kernel, grid=(steps,), in_specs=[pl.BlockSpec((row...  14.2 us
    pallas_call x1, Pallas kernels, products(): pl.pallas_call(product_kernel, grid_spec=pltpu.PrefetchScalarGridSpec(num...  11.6 us
    ppermute x1, starting transfers between devices, local(): take = lax.ppermute(give, 'c', SWAP)  10.9 us
    pallas_call x1, Pallas kernels, hidden_stage(): pl.pallas_call(hidden_kernel, grid=(rows // part,), in_specs=[pl.BlockSpe...  10.8 us
  transfers between devices with their start and end apart: 31, of which 17 were waited for; matrix products, arithmetic and copies ran while one was open for 11% of the time, Pallas kernels for 16%

commit v1 on v0

--- a/solution.py
+++ b/solution.py
@@ -43,7 +43,7 @@
 
 
 def project_kernel(
-    rel, choose, x, dy, gate_w, up_w, down_w, a_g, a_u, out_f, pre, coef, own, acc_x, acc_dy
+    rel, choose, x, dy, tall_w, wide_w, pre, coef, own, acc_x, acc_dy
 ):
     j = pl.program_id(0)
 
@@ -53,9 +53,9 @@
         acc_dy[...] = jnp.zeros_like(acc_dy)
 
     xv, dv = x[...], dy[...]
-    acc_x[:, : 2 * LANES] += dot(xv, jnp.concatenate([gate_w[...], up_w[...]], axis=1))
-    acc_x[:, 2 * LANES :] += dot_nt(xv, jnp.concatenate([a_g[...], a_u[...]], axis=0))
-    acc_dy[...] += dot_nt(dv, jnp.concatenate([down_w[...], out_f[...]], axis=0))
+    acc_x[:, : 2 * LANES] += dot(xv, tall_w[...])
+    acc_x[:, 2 * LANES :] += dot_nt(xv, wide_w[2 * LANES :, :])
+    acc_dy[...] += dot_nt(dv, wide_w[: 2 * LANES, :])
     cap = choose.shape[0]
     own[:cap, :] = dot(choose[...], xv).astype(BF)
     own[cap:, :] = dot(choose[...], dv).astype(BF)
@@ -78,13 +78,11 @@
         coef[...] = dot(choose[...], packed.astype(BF)).astype(BF)
 
 
-def project(rel, choose, both, gate_w, up_w, down_w, a_g, a_u, out_f):
+def project(rel, choose, both, tall_w, wide_w):
     rows, d = both.shape[0], both.shape[1] // 2
     cap = choose.shape[0]
     width = 1024
     steps = d // width
-    tall = pl.BlockSpec((width, LANES), lambda j: (j, 0))
-    wide = pl.BlockSpec((LANES, width), lambda j: (0, j))
     return pl.pallas_call(
         project_kernel,
         grid=(steps,),
@@ -93,12 +91,8 @@
             pl.BlockSpec((cap, rows), lambda j: (0, 0)),
             pl.BlockSpec((rows, width), lambda j: (0, j)),
             pl.BlockSpec((rows, width), lambda j: (0, j + steps)),
-            tall,
-            tall,
-            wide,
-            wide,
-            wide,
-            wide,
+            pl.BlockSpec((width, tall_w.shape[1]), lambda j: (j, 0)),
+            pl.BlockSpec((wide_w.shape[0], width), lambda j: (0, j)),
         ],
         out_specs=[
             pl.BlockSpec((rows, 3 * LANES), lambda j: (0, 0)),
@@ -113,7 +107,7 @@
         scratch_shapes=[pltpu.VMEM((rows, 4 * LANES), F32), pltpu.VMEM((rows, 2 * LANES), F32)],
         compiler_params=params(32),
         name="project",
-    )(rel, choose, both, both, gate_w, up_w, down_w, a_g, a_u, out_f)
+    )(rel, choose, both, both, tall_w, wide_w)
 
 
 def hidden_kernel(tenant, pos, pos_row, table, pre, b_g, b_u, a_d, values, placed, partial):
@@ -170,7 +164,7 @@
 
 def hidden_stage(tenant, pos, pos_row, table, pre, b_g, b_u, a_d):
     rows = pre.shape[0]
-    part = 128
+    part = 256
     whole = lambda a: pl.BlockSpec(a.shape, lambda j: (0, 0))
     spots = table.shape[0]
     return pl.pallas_call(
@@ -226,35 +220,35 @@
     )(rel, choose_t, low, order_m, order_i, values)
 
 
-def product_kernel(core, left, other, down_w, out_f, gate_w, up_w, a_g, a_u, near, side, *outs):
+def product_kernel(core, left, other, tall_w, wide_w, near, side, *outs):
     del core
     m, i = 2 * LANES, 4 * LANES
-    total = dot(left[:, :m], jnp.concatenate([down_w[...], out_f[...]], axis=0))
+    total = dot(left[:, :m], wide_w[:m, :])
     total += dot(other[:, :m], near[:m, :])
     mixed = total.astype(BF)
-    total = dot_nt(left[:, m:i], jnp.concatenate([gate_w[...], up_w[...]], axis=1))
-    total += dot(left[:, i:], jnp.concatenate([a_g[...], a_u[...]], axis=0))
+    total = dot_nt(left[:, m:i], tall_w[...])
+    total += dot(left[:, i:], wide_w[m:, :])
     total += dot_nt(other[:, m:i], side[...])
     total += dot(other[:, i:], near[m:, :])
     back = total.astype(BF)
-    n = mixed.shape[0] // 4
+    n = mixed.shape[0] // RING
     h = n // 2
-    for at, value in ((0, mixed), (7, back)):
-        for k, (first, count) in enumerate(
-            ((0, n), (n, h), (n + h, h), (2 * n, h), (2 * n + h, h), (3 * n, h), (3 * n + h, h))
-        ):
-            outs[at + k][...] = value[first : first + count, :]
-
-
-def products(core, left, other, down_w, out_f, gate_w, up_w, a_g, a_u, near, side):
+    for far0, far1, rest, value in ((*outs[:3], mixed), (*outs[3:], back)):
+        far0[...] = value[2 * n : 2 * n + h, :]
+        far1[...] = value[2 * n + h : 3 * n, :]
+        rest[: 2 * n, :] = value[: 2 * n, :]
+        rest[2 * n :, :] = value[3 * n :, :]
+
+
+def products(core, left, other, tall_w, wide_w, near, side):
     rows, half = left.shape[0], near.shape[1]
     width = 512
     steps = half // width
-    n = rows // 4
+    n = rows // RING
     whole = lambda a: pl.BlockSpec(a.shape, lambda j, c: (0, 0))
-    wide = pl.BlockSpec((LANES, width), lambda j, c: (0, c[0] * steps + j))
-    tall = pl.BlockSpec((width, LANES), lambda j, c: (c[0] * steps + j, 0))
-    counts = 2 * [n, n // 2, n // 2, n // 2, n // 2, n // 2, n // 2]
+    wide = lambda a, k: pl.BlockSpec((a.shape[0], width), lambda j, c: (0, c[0] * k + j))
+    tall = lambda a, k: pl.BlockSpec((width, a.shape[1]), lambda j, c: (c[0] * k + j, 0))
+    counts = 2 * [n // 2, n // 2, 3 * n]
     return pl.pallas_call(
         product_kernel,
         grid_spec=pltpu.PrefetchScalarGridSpec(
@@ -263,21 +257,17 @@
             in_specs=[
                 whole(left),
                 whole(other),
-                wide,
-                wide,
-                tall,
-                tall,
-                wide,
-                wide,
-                pl.BlockSpec((near.shape[0], width), lambda j, c: (0, j)),
-                pl.BlockSpec((width, side.shape[1]), lambda j, c: (j, 0)),
+                tall(tall_w, steps),
+                wide(wide_w, steps),
+                wide(near, 0),
+                tall(side, 0),
             ],
             out_specs=[pl.BlockSpec((k, width), lambda j, c: (0, j)) for k in counts],
         ),
         out_shape=[jax.ShapeDtypeStruct((k, half), BF) for k in counts],
         compiler_params=params(40),
         name="products",
-    )(core, left, other, down_w, out_f, gate_w, up_w, a_g, a_u, near, side)
+    )(core, left, other, tall_w, wide_w, near, side)
 
 
 def tenant_kernel(rel_tenant, values, out_bg, out_bu, out_ad):
@@ -350,19 +340,21 @@
     return total.astype(BF)
 
 
-def first_step(a, b, axes, *beside):
+def first_step(a, b, axes):
     sent = []
     for p, axis in ((a, axes[0]), (b, axes[1])):
-        sent += [lax.ppermute(p[3], axis, UP), lax.ppermute(p[4], axis, DOWN)]
-    done = lax.optimization_barrier((*sent, *beside))
-    return done[:4], done[4:]
+        sent += [lax.ppermute(p[0], axis, UP), lax.ppermute(p[1], axis, DOWN)]
+    return lax.optimization_barrier(sent)
 
 
 def second_start(a, b, axes, sent):
     moved = []
     for k, (p, axis) in enumerate(((a, axes[0]), (b, axes[1]))):
-        right = jnp.concatenate([add(p[1], sent[2 * k]), p[2]], axis=0)
-        left = jnp.concatenate([p[5], add(p[6], sent[2 * k + 1])], axis=0)
+        n = p[2].shape[0] // 3
+        h = n // 2
+        right, left = p[2][n : 2 * n], p[2][2 * n :]
+        right = jnp.concatenate([add(right[:h], sent[2 * k]), right[h:]], axis=0)
+        left = jnp.concatenate([left[:h], add(left[h:], sent[2 * k + 1])], axis=0)
         moved += [lax.ppermute(right, axis, UP), lax.ppermute(left, axis, DOWN)]
     return moved
 
@@ -370,34 +362,16 @@
 def second_end(a, b, moved, *beside):
     done = lax.optimization_barrier((*moved, *beside))
     moved, beside = done[:4], done[4:]
-    return add(a[0], moved[0], moved[1]), add(b[0], moved[2], moved[3]), beside
-
-
-def ring_near(v, axis):
-    return lax.ppermute(v, axis, UP), lax.ppermute(v, axis, DOWN)
-
-
-def ring_far(left, right, axis):
-    h = left.shape[0] // 2
-    return lax.ppermute(left[:h], axis, UP), lax.ppermute(right[h:], axis, DOWN)
-
-
-def ring_join(v, near, far):
-    return jnp.stack([v, *near, jnp.concatenate(far, axis=0)], axis=0)
-
-
-def sevenths(v):
-    n = v.shape[0] // 4
-    h = n // 2
-    cut = lambda first, count: v[first : first + count]
+    own = lambda p: p[2][: p[2].shape[0] // 3]
+    return add(own(a), moved[0], moved[1]), add(own(b), moved[2], moved[3]), beside
+
+
+def in_pieces(v):
+    n = v.shape[0] // RING
     return (
-        cut(0, n),
-        cut(n, h),
-        cut(n + h, h),
-        cut(2 * n, h),
-        cut(2 * n + h, h),
-        cut(3 * n, h),
-        cut(3 * n + h, h),
+        v[2 * n : 2 * n + n // 2],
+        v[2 * n + n // 2 : 3 * n],
+        jnp.concatenate([v[: 2 * n], v[3 * n :]], axis=0),
     )
 
 
@@ -453,13 +427,11 @@
     choose = here(all_choose).astype(BF)
     rel = slots - per_owner * blk
 
+    tall_w = jnp.concatenate([gate_weight, up_weight], axis=1)
+    wide_w = jnp.concatenate([down_weight, out_f, a_g, a_u], axis=0)
     far = (1 - c_at) * half
-    cut_wide = lambda v: lax.dynamic_slice_in_dim(v, far, half, 1)
-    cut_tall = lambda v: lax.dynamic_slice_in_dim(v, far, half, 0)
-    near = jnp.concatenate([cut_wide(v) for v in (down_weight, out_f, a_g, a_u)], axis=0)
-    side = jnp.concatenate([cut_tall(gate_weight), cut_tall(up_weight)], axis=1)
-    near = lax.ppermute(near, "c", SWAP)
-    side = lax.ppermute(side, "c", SWAP)
+    near = lax.ppermute(lax.dynamic_slice_in_dim(wide_w, far, half, 1), "c", SWAP)
+    side = lax.ppermute(lax.dynamic_slice_in_dim(tall_w, far, half, 0), "c", SWAP)
 
     j = jnp.arange(group_rows, dtype=jnp.int32)
     inner = j % (CORES * own_rows)
@@ -472,18 +444,15 @@
     both = jnp.concatenate([tokens, cotangent], axis=1)
     both = lax.all_gather(both, BLK, axis=0, tiled=True)
     rel = rel[:, None]
-    pre, coef, own = project(
-        rel, choose, both, gate_weight, up_weight, down_weight, a_g, a_u, out_f
-    )
-    own_near = ring_near(own, "y")
+    both, tall_w, wide_w, near, side = lax.optimization_barrier((both, tall_w, wide_w, near, side))
+    pre, coef, own = project(rel, choose, both, tall_w, wide_w)
+    all_own = lax.all_gather(own, "y", axis=0)
     copies = jnp.broadcast_to(coef[:, : 3 * RANK], (blk_count, cap, 3 * RANK))
     table = lax.all_to_all(copies, BLK, split_axis=0, concat_axis=0, tiled=True)
     table = jnp.pad(table.reshape(blk_count * cap, 3 * RANK), ((0, 0), (0, LANES - 3 * RANK)))
     values, placed = hidden_stage(
         tenants[:, None], position[:, None], position[None, :], table, pre, b_g, b_u, a_d
     )
-    placed, *own_near = lax.optimization_barrier((placed, *own_near))
-    own_far = ring_far(*own_near, "y")
     terms = placed[:, : 3 * RANK].reshape(blk_count, cap, 3 * RANK)
     terms = lax.all_to_all(terms, BLK, split_axis=0, concat_axis=0, tiled=True)
     low = jnp.sum(terms.astype(F32), axis=0).astype(BF)
@@ -491,38 +460,20 @@
     left = left_stage(rel, jnp.transpose(choose), low[:cap], order_m, order_i, values)
     other = lax.ppermute(left, "c", SWAP)
     packed = jnp.concatenate([values, low.reshape(-1, 4 * LANES)], axis=0)
-    left, other, packed, *own_far = lax.optimization_barrier((left, other, packed, *own_far))
-    packed_near = ring_near(packed, "y")
+    left, other, packed, all_own = lax.optimization_barrier((left, other, packed, all_own))
+    packed = lax.all_gather(packed, "y", axis=0)
     pieces = products(
-        c_at.reshape(1).astype(jnp.int32),
-        left,
-        other,
-        down_weight,
-        out_f,
-        gate_weight,
-        up_weight,
-        a_g,
-        a_u,
-        near,
-        side,
-    )
-    pieces = (pieces[:7], pieces[7:])
-    sent, packed_near = first_step(*pieces, ("x", "z"), *packed_near)
+        c_at.reshape(1).astype(jnp.int32), left, other, tall_w, wide_w, near, side
+    )
+    pieces = (pieces[:3], pieces[3:])
+    sent = first_step(*pieces, ("x", "z"))
     moved = second_start(*pieces, ("x", "z"), sent)
-    packed_far = ring_far(*packed_near, "y")
-
-    all_own = ring_join(own, own_near, own_far)
-    packed = ring_join(packed, packed_near, packed_far)
-    turn = (grp + jnp.array([0, -1, 1, 2], jnp.int32)) % grp_count
-    turned = lambda v: jnp.sum(
-        jnp.where((turn[:, None] == jnp.arange(grp_count, dtype=jnp.int32))[:, :, None], v[None], 0), 1
-    )
     low_all = packed[:, group_rows:, :].astype(F32)
     low_all = low_all.reshape(grp_count, -1, LANES)[:, :cap, : 3 * RANK]
     slots_dev = per_owner // grp_count
     wanted = grp * slots_dev + jnp.arange(slots_dev, dtype=jnp.int32)
     weights = jnp.where(
-        (turned(own_slot)[None] == wanted[:, None, None])[:, None],
+        (own_slot[None] == wanted[:, None, None])[:, None],
         jnp.transpose(low_all, (2, 0, 1))[None],
         0.0,
     )
@@ -531,11 +482,11 @@
     weights = jnp.concatenate([weights[1], weights[2], 2.0 * weights[0]], axis=0).astype(BF)
     by_slot = slot_gradients(weights, all_own)
     tenant_dev = tenant_count // grp_count
-    by_tenant = tenant_gradients(turned(all_tenants) - grp * tenant_dev, packed, tenant_dev)
+    by_tenant = tenant_gradients(all_tenants - grp * tenant_dev, packed, tenant_dev)
 
     *sums, grads = second_end(*pieces, moved, *by_slot, *by_tenant)
-    pieces = (sevenths(sums[0]), sevenths(sums[1]))
-    sent, _ = first_step(*pieces, ("z", "x"))
+    pieces = (in_pieces(sums[0]), in_pieces(sums[1]))
+    sent = first_step(*pieces, ("z", "x"))
     moved = second_start(*pieces, ("z", "x"), sent)
     *sums, _ = second_end(*pieces, moved)
     stacked = jnp.stack([v.reshape(CORES, own_rows, half) for v in sums], axis=1)

time: 292 us -> 258 us (0.88)
  waiting for transfers between devices: 121 us -> 101 us
  starting transfers between devices: 52.6 us -> 38.9 us
  local copies, waits for them, and re-layouts: 26.4 us -> 32.7 us
  other arithmetic: 28.7 us -> 24.8 us
    ppermute x18 -> x10, waiting for transfers between devices: 27.3 us -> 15.4 us  [the longest x8 13.6 us: first_step(): sent += [lax.ppermute(p[0], axis, UP), lax.ppermute(p[1], axis, DOWN)]]
    ppermute x18 -> x10, starting transfers between devices: 23.7 us -> 13.5 us  [the longest x8 10.9 us: first_step(): sent += [lax.ppermute(p[0], axis, UP), lax.ppermute(p[1], axis, DOWN)]]
    unnamed x53 -> x48, local copies, waits for them, and re-layouts: 17.8 us -> 25.3 us
    all_gather x1, waiting for transfers between devices: 64.6 us -> 57.6 us  [local(): both = lax.all_gather(both, BLK, axis=0, tiled=True)]
    another operation x6 -> x2, other arithmetic: 5.22 us -> 0.02 us  [the longest x4 5.21 us: ring_join(): return jnp.stack([v, *near, jnp.concatenate(far, axis=0)], axis=0)]
    ppermute x1, starting transfers between devices: 10.9 us -> 6.73 us  [local(): take = lax.ppermute(give, 'c', SWAP)]
    slice x6 -> x4, local copies, waits for them, and re-layouts: 3.89 us -> 0.24 us  [second_start(): left = jnp.concatenate([left[:h], add(left[h:], sent[2 * k + 1])], axis=0)]
    concatenate x10 -> x9, other arithmetic: 8.4 us -> 5.54 us  [the longest x1 4.14 us: local(): wide_w = jnp.concatenate([down_weight, out_f, a_g, a_u], axis=0)]
  transfers between devices with their start and end apart: 31 -> 25, of which waited for: 17 -> 15; matrix products, arithmetic and copies ran while one was open for 11% -> 11% of each run, Pallas kernels for 16% -> 12%
where the time goes in v1:
time: 258 us; the launch traced here: 256 us
  waiting for transfers between devices  101 us (39%)
  Pallas kernels  45.1 us (17%)
  starting transfers between devices  38.9 us (15%)
  local copies, waits for them, and re-layouts  32.7 us (13%)
  other arithmetic  24.8 us (10%)
  between operations  14.3 us (6%)
    all_gather x1, waiting for transfers between devices, local(): both = lax.all_gather(both, BLK, axis=0, tiled=True)  57.6 us
    unnamed x48, local copies, waits for them, and re-layouts  25.3 us
    ppermute x8, waiting for transfers between devices, second_start(): moved += [lax.ppermute(right, axis, UP), lax.ppermute(left, axis, DOWN)]  15 us
    pallas_call x1, Pallas kernels, project(): pl.pallas_call(project_kernel, grid=(steps,), in_specs=[pl.BlockSpec((row...  14.1 us
    ppermute x8, waiting for transfers between devices, first_step(): sent += [lax.ppermute(p[0], axis, UP), lax.ppermute(p[1], axis, DOWN)]  13.6 us
    pallas_call x1, Pallas kernels, products(): pl.pallas_call(product_kernel, grid_spec=pltpu.PrefetchScalarGridSpec(num...  11.2 us
    ppermute x8, starting transfers between devices, first_step(): sent += [lax.ppermute(p[0], axis, UP), lax.ppermute(p[1], axis, DOWN)]  10.9 us
    pallas_call x1, Pallas kernels, hidden_stage(): pl.pallas_call(hidden_kernel, grid=(rows // part,), in_specs=[pl.BlockSpe...  9.05 us
  transfers between devices with their start and end apart: 25, of which 15 were waited for; matrix products, arithmetic and copies ran while one was open for 11% of the time, Pallas kernels for 12%

profile of v1, /device:TPU:1, one launch (start us, length us, event | category | flops | bytes accessed | tf_op | source)
XLA Modules:
  0.0 256.5 jit_solution(6988415944810485180)
XLA Ops:
  9.2 4.1 %pad_maximum_fusion.wide_w = bf16[512,8192]{1,0:T(8,128)(2,1)S(1)} fusion(bf16[128,8192]{1,0:T(8,128)(2,1)} %bitcast.53, bf16[128,8192]{1,0:T(8,128)(2,1)} %bitcast.54, bf16[128,8192]{1,0:T(8,128)(2,1)} %bitcast.55, bf16[128,8192]{1,0:T(8,128)(2,1)} %param.17), kind=kLoop, calls=%fused_computation | loop fusion | flops 33554432 | bytes 16777216 | tf_op jit(solution)/shard_map/concatenate | solution.py:431
  15.7 2.4 copy-done
  29.5 57.6 %all-gather.6.cloned.1.call-done.x.dy = bf16[512,16384]{1,0:T(8,128)(2,1)} async-done(((bf16[16,16384]{1,0:T(8,128)(2,1)}), bf16[512,16384]{1,0:T(8,128)(2,1)}) %all-gather.6.cloned.1.call-update) | async-done | bytes 16777232 | tf_op jit(solution)/shard_map/all_gather | solution.py:445
  87.1 3.4 %copy-done.1 = bf16[512,8192]{1,0:T(8,128)(2,1)S(1)} copy-done((bf16[512,8192]{1,0:T(8,128)(2,1)S(1)}, bf16[512,8192]{1,0:T(8,128)(2,1)}, u32[]{:S(2)}) %copy-start.1) | copy-done | bytes 8388632
  92.7 14.1 %project.1 = (f32[512,384]{1,0:T(8,128)S(1)}, bf16[32,128]{1,0:T(8,128)(2,1)S(1)}, bf16[64,8192]{1,0:T(8,128)(2,1)}) custom-call(s32[512,1]{1,0:T(8,128)S(1)} %copy.35.rel, bf16[32,512]{1,0:T(8,128)(2,1)S(1)} %copy.32.choose, bf16[512,16384]{1,0:T(8,128)(2,1)} %all-gather.6.cloned.1.call-done.x.dy, bf16[512,16384]{1,0:T(8,128)(2,1)} %all-gather.6.cloned.1.call-done.x.dy, ...), custom_call_target="tpu_custom_call" | custom-call | tf_op jit(solution)/shard_map/project/pallas_call | solution.py:86
  109.7 5.4 %all-to-all-start = ((bf16[32,2,768]{2,1,0:T(2,128)(2,1)}), bf16[32,2,768]{2,1,0:T(2,128)(2,1)}, u32[]{:S(2)}, u32[]{:S(2)}) async-start(bf16[32,2,768]{2,1,0:T(2,128)(2,1)} %reshape.492), calls=%async_computation | async-start | bytes 196608 | tf_op jit(solution)/shard_map/all_to_all | solution.py:451
  116.4 6.3 %all-to-all-done = bf16[32,2,768]{2,1,0:T(2,128)(2,1)} async-done(((bf16[32,2,768]{2,1,0:T(2,128)(2,1)}), bf16[32,2,768]{2,1,0:T(2,128)(2,1)}, u32[]{:S(2)}, u32[]{:S(2)}) %all-to-all-start) | async-done | bytes 98336 | tf_op jit(solution)/shard_map/all_to_all | solution.py:451
  128.7 9.1 %hidden_stage.1 = (bf16[512,512]{1,0:T(8,128)(2,1)S(1)}, bf16[1024,128]{1,0:T(8,128)(2,1)S(1)}) custom-call(s32[512,1]{1,0:T(8,128)S(1)} %copy.33.tenant, s32[512,1]{1,0:T(8,128)S(1)} %copy.34.pos, s32[1,512]{1,0:T(1,128)S(1)} %fusion.37.pos_row, bf16[1024,128]{1,0:T(8,128)(2,1)S(1)} %pad.8.table, f32[512,384]{1,0:T(8,128)S(1)} %copy-done.15, ...), custom_call_target="tpu_custom_call" | custom-call | tf_op jit(solution)/shard_map/hidden_stage/pallas_call | solution.py:170
  139.6 3.9 %all-to-all-start.1 = ((bf16[32,2,768]{2,1,0:T(2,128)(2,1)}), bf16[32,2,768]{2,1,0:T(2,128)(2,1)S(1)}, u32[]{:S(2)}, u32[]{:S(2)}) async-start(bf16[32,2,768]{2,1,0:T(2,128)(2,1)} %reshape.494), calls=%async_computation.1 | async-start | bytes 196608 | tf_op jit(solution)/shard_map/all_to_all | solution.py:457
  145.8 5.3 %all-to-all-done.1 = bf16[32,2,768]{2,1,0:T(2,128)(2,1)S(1)} async-done(((bf16[32,2,768]{2,1,0:T(2,128)(2,1)}), bf16[32,2,768]{2,1,0:T(2,128)(2,1)S(1)}, u32[]{:S(2)}, u32[]{:S(2)}) %all-to-all-start.1) | async-done | bytes 98336 | tf_op jit(solution)/shard_map/all_to_all | solution.py:457
  157.6 11.2 %products.1 = (bf16[64,4096]{1,0:T(8,128)(2,1)S(1)}, bf16[64,4096]{1,0:T(8,128)(2,1)S(1)}, bf16[384,4096]{1,0:T(8,128)(2,1)S(1)}, bf16[64,4096]{1,0:T(8,128)(2,1...) custom-call(s32[1]{0:T(128)} %bitcast.core, bf16[512,768]{1,0:T(8,128)(2,1)S(1)} %left_stage.1.left, ...), custom_call_target="tpu_custom_call" | custom-call | tf_op jit(solution)/shard_map/products/pallas_call | solution.py:252
  169.2 2.4 collective-permute-start.4
  171.8 2.5 collective-permute-start.6
  174.4 9.2 %collective-permute-done.3 = bf16[64,4096]{1,0:T(8,128)(2,1)S(1)} collective-permute-done((bf16[64,4096]{1,0:T(8,128)(2,1)S(1)}, bf16[64,4096]{1,0:T(8,128)(2,1)S(1)}, u32[]{:S(2)}, u32[]{:S(2)}) %collective-permute-start.3) | collective-permute-done | bytes 524320 | tf_op jit(solution)/shard_map/ppermute | solution.py:346
  186.0 2.4 collective-permute-start.10
  194.5 5.8 %tenant_gradients.1 = (f32[1024,128]{1,0:T(8,128)}, f32[1024,128]{1,0:T(8,128)}, f32[1024,128]{1,0:T(8,128)}) custom-call(s32[4,512]{1,0:T(4,128)S(1)} %broadcast_subtract_fusion.rel_tenant, bf16[4,528,512]{2,1,0:T(8,128)(2,1)S(1)} %bitcast.46), custom_call_target="tpu_custom_call" | custom-call | tf_op jit(solution)/shard_map/tenant_gradients/pallas_call | solution.py:298
  202.6 4.0 %slot_gradients.1 = (f32[32,8192]{1,0:T(8,128)}, f32[32,8192]{1,0:T(8,128)}, f32[32,8192]{1,0:T(8,128)}) custom-call(bf16[96,128]{1,0:T(8,128)(2,1)S(1)} %pad_maximum_fusion.11.weights, bf16[4,64,8192]{2,1,0:T(8,128)(2,1)S(1)} %bitcast.44), custom_call_target="tpu_custom_call" | custom-call | tf_op jit(solution)/shard_map/slot_gradients/pallas_call | solution.py:322
  206.6 2.7 %collective-permute-done.10 = bf16[128,4096]{1,0:T(8,128)(2,1)} collective-permute-done((bf16[128,4096]{1,0:T(8,128)(2,1)S(1)}, bf16[128,4096]{1,0:T(8,128)(2,1)}, u32[]{:S(2)}, u32[]{:S(2)}) %collective-permute-start.10) | collective-permute-done | bytes 1048608 | tf_op jit(solution)/shard_map/ppermute | solution.py:358
  209.3 3.1 %collective-permute-done.9 = bf16[128,4096]{1,0:T(8,128)(2,1)} collective-permute-done((bf16[128,4096]{1,0:T(8,128)(2,1)S(1)}, bf16[128,4096]{1,0:T(8,128)(2,1)}, u32[]{:S(2)}, u32[]{:S(2)}) %collective-permute-start.9) | collective-permute-done | bytes 1048608 | tf_op jit(solution)/shard_map/ppermute | solution.py:358
  217.2 2.7 %collective-permute-start.14 = (bf16[16,4096]{1,0:T(8,128)(2,1)S(1)}, bf16[16,4096]{1,0:T(8,128)(2,1)S(1)}, u32[]{:S(2)}, u32[]{:S(2)}) collective-permute-start(bf16[16,4096]{1,0:T(8,128)(2,1)S(1)} %get-tuple-element.116), channel_id=1, source_target_pairs={{0,96},{32,0},{64,32},{96,64},{1,97},{33,1},{65,33},{97,65},{2,98}... | collective-permute-start | bytes 393224 | tf_op jit(solution)/shard_map/ppermute | solution.py:346
  222.4 2.7 %collective-permute-start.12 = (bf16[16,4096]{1,0:T(8,128)(2,1)S(1)}, bf16[16,4096]{1,0:T(8,128)(2,1)S(1)}, u32[]{:S(2)}, u32[]{:S(2)}) collective-permute-start(bf16[16,4096]{1,0:T(8,128)(2,1)S(1)} %get-tuple-element.122), channel_id=1, source_target_pairs={{0,24},{8,0},{16,8},{24,16},{1,25},{9,1},{17,9},{25,17},{2,26},{10... | collective-permute-start | bytes 393224 | tf_op jit(solution)/shard_map/ppermute | solution.py:346
  229.2 2.7 %collective-permute-start.16 = (bf16[32,4096]{1,0:T(8,128)(2,1)S(1)}, bf16[32,4096]{1,0:T(8,128)(2,1)}, u32[]{:S(2)}, u32[]{:S(2)}) collective-permute-start(bf16[32,4096]{1,0:T(8,128)(2,1)S(1)} %pad_maximum_fusion.8), channel_id=1, source_target_pairs={{0,24},{8,0},{16,8},{24,16},{1,25},{9,1},{17,9},{25,17},{2,26},{10... | collective-permute-start | bytes 786440 | tf_op jit(solution)/shard_map/ppermute | solution.py:358
  235.3 3.6 %collective-permute-done.15 = bf16[32,4096]{1,0:T(8,128)(2,1)} collective-permute-done((bf16[32,4096]{1,0:T(8,128)(2,1)S(1)}, bf16[32,4096]{1,0:T(8,128)(2,1)}, u32[]{:S(2)}, u32[]{:S(2)}) %collective-permute-start.15) | collective-permute-done | bytes 262176 | tf_op jit(solution)/shard_map/ppermute | solution.py:358
  241.1 6.7 %collective-permute-start.19 = (bf16[2,16,4096]{2,1,0:T(8,128)(2,1)S(1)}, bf16[2,16,4096]{2,1,0:T(8,128)(2,1)S(1)}, u32[]{:S(2)}, u32[]{:S(2)}) collective-permute-start(bf16[2,16,4096]{2,1,0:T(8,128)(2,1)S(1)} %get-tuple-element.129), channel_id=1, source_target_pairs={{0,4},{4,0},{1,5},{5,1},{2,6},{6,2},{3,7},{7,3},{8,12},{12,8},{9,1... | collective-permute-start | bytes 786440 | tf_op jit(solution)/shard_map/ppermute | solution.py:495
  (151 shorter events, 68.8 us)
Async XLA Ops:
  7.2 79.9 %all-gather.6.cloned.1.call-start = ((), (), s32[]{:S(2)}) async-start(), calls=%async_computation.2 | async-start | bytes 17301504 | tf_op jit(solution)/shard_map/all_gather | solution.py:445
  9.1 148.5 %all-gather.8.cloned.1.call-start = ((), (), s32[]{:S(2)}) async-start(), calls=%async_computation.3 | async-start | bytes 5242880 | tf_op jit(solution)/shard_map/all_gather | solution.py:449
  18.1 11.4 %collective-permute-start = (bf16[512,4096]{1,0:T(8,128)(2,1)}, bf16[512,4096]{1,0:T(8,128)(2,1)}, u32[]{:S(2)}, u32[]{:S(2)}) collective-permute-start(bf16[512,4096]{1,0:T(8,128)(2,1)} %constant_dynamic-slice_fusion.1), channel_id=1, source_target_pairs={{0,4},{4,0},{1,5},{5,1},{2,6},{6,2},{3,7},{7,3},{8,12},{12,8},{9,1... | collective-permute-start | bytes 12582920 | tf_op jit(solution)/shard_map/ppermute | solution.py:433
  23.1 6.4 %collective-permute-start.1 = (bf16[4096,256]{1,0:T(8,128)(2,1)}, bf16[4096,256]{1,0:T(8,128)(2,1)S(1)}, u32[]{:S(2)}, u32[]{:S(2)}) collective-permute-start(bf16[4096,256]{1,0:T(8,128)(2,1)} %constant_dynamic-slice_fusion), channel_id=1, source_target_pairs={{0,4},{4,0},{1,5},{5,1},{2,6},{6,2},{3,7},{7,3},{8,12},{12,8},{9,1... | collective-permute-start | bytes 6291464 | tf_op jit(solution)/shard_map/ppermute | solution.py:434
  109.7 12.9 %all-to-all-start = ((bf16[32,2,768]{2,1,0:T(2,128)(2,1)}), bf16[32,2,768]{2,1,0:T(2,128)(2,1)}, u32[]{:S(2)}, u32[]{:S(2)}) async-start(bf16[32,2,768]{2,1,0:T(2,128)(2,1)} %reshape.492), calls=%async_computation | async-start | bytes 196608 | tf_op jit(solution)/shard_map/all_to_all | solution.py:451
  139.6 11.5 %all-to-all-start.1 = ((bf16[32,2,768]{2,1,0:T(2,128)(2,1)}), bf16[32,2,768]{2,1,0:T(2,128)(2,1)S(1)}, u32[]{:S(2)}, u32[]{:S(2)}) async-start(bf16[32,2,768]{2,1,0:T(2,128)(2,1)} %reshape.494), calls=%async_computation.1 | async-start | bytes 196608 | tf_op jit(solution)/shard_map/all_to_all | solution.py:457
  143.5 48.3 %all-gather.10.cloned.1.call-start = ((), (), s32[]{:S(2)}) async-start(), calls=%async_computation.4 | async-start | bytes 2703360 | tf_op jit(solution)/shard_map/all_gather | solution.py:464
  168.8 14.8 %collective-permute-start.3 = (bf16[64,4096]{1,0:T(8,128)(2,1)S(1)}, bf16[64,4096]{1,0:T(8,128)(2,1)S(1)}, u32[]{:S(2)}, u32[]{:S(2)}) collective-permute-start(bf16[64,4096]{1,0:T(8,128)(2,1)S(1)} %get-tuple-element.69), channel_id=1, source_target_pairs={{0,32},{32,64},{64,96},{96,0},{1,33},{33,65},{65,97},{97,1},{2,34}... | collective-permute-start | bytes 1572872 | tf_op jit(solution)/shard_map/ppermute | solution.py:346
  169.2 14.5 %collective-permute-start.4 = (bf16[64,4096]{1,0:T(8,128)(2,1)S(1)}, bf16[64,4096]{1,0:T(8,128)(2,1)S(1)}, u32[]{:S(2)}, u32[]{:S(2)}) collective-permute-start(bf16[64,4096]{1,0:T(8,128)(2,1)S(1)} %get-tuple-element.70), channel_id=1, source_target_pairs={{0,96},{32,0},{64,32},{96,64},{1,97},{33,1},{65,33},{97,65},{2,98}... | collective-permute-start | bytes 1572872 | tf_op jit(solution)/shard_map/ppermute | solution.py:346
  171.6 14.1 %collective-permute-start.5 = (bf16[64,4096]{1,0:T(8,128)(2,1)S(1)}, bf16[64,4096]{1,0:T(8,128)(2,1)S(1)}, u32[]{:S(2)}, u32[]{:S(2)}) collective-permute-start(bf16[64,4096]{1,0:T(8,128)(2,1)S(1)} %get-tuple-element.71), channel_id=1, source_target_pairs={{0,8},{8,16},{16,24},{24,0},{1,9},{9,17},{17,25},{25,1},{2,10},{10... | collective-permute-start | bytes 1572872 | tf_op jit(solution)/shard_map/ppermute | solution.py:346
  171.8 13.9 %collective-permute-start.6 = (bf16[64,4096]{1,0:T(8,128)(2,1)S(1)}, bf16[64,4096]{1,0:T(8,128)(2,1)S(1)}, u32[]{:S(2)}, u32[]{:S(2)}) collective-permute-start(bf16[64,4096]{1,0:T(8,128)(2,1)S(1)} %get-tuple-element.72), channel_id=1, source_target_pairs={{0,24},{8,0},{16,8},{24,16},{1,25},{9,1},{17,9},{25,17},{2,26},{10... | collective-permute-start | bytes 1572872 | tf_op jit(solution)/shard_map/ppermute | solution.py:346
  186.0 23.3 %collective-permute-start.10 = (bf16[128,4096]{1,0:T(8,128)(2,1)S(1)}, bf16[128,4096]{1,0:T(8,128)(2,1)}, u32[]{:S(2)}, u32[]{:S(2)}) collective-permute-start(bf16[128,4096]{1,0:T(8,128)(2,1)S(1)} %pad_maximum_fusion.4), channel_id=1, source_target_pairs={{0,24},{8,0},{16,8},{24,16},{1,25},{9,1},{17,9},{25,17},{2,26},{10... | collective-permute-start | bytes 3145736 | tf_op jit(solution)/shard_map/ppermute | solution.py:358
  188.5 24.0 %collective-permute-start.9 = (bf16[128,4096]{1,0:T(8,128)(2,1)S(1)}, bf16[128,4096]{1,0:T(8,128)(2,1)}, u32[]{:S(2)}, u32[]{:S(2)}) collective-permute-start(bf16[128,4096]{1,0:T(8,128)(2,1)S(1)} %pad_maximum_fusion.3), channel_id=1, source_target_pairs={{0,8},{8,16},{16,24},{24,0},{1,9},{9,17},{17,25},{25,1},{2,10},{10... | collective-permute-start | bytes 3145736 | tf_op jit(solution)/shard_map/ppermute | solution.py:358
  188.9 23.5 %collective-permute-start.8 = (bf16[128,4096]{1,0:T(8,128)(2,1)S(1)}, bf16[128,4096]{1,0:T(8,128)(2,1)}, u32[]{:S(2)}, u32[]{:S(2)}) collective-permute-start(bf16[128,4096]{1,0:T(8,128)(2,1)S(1)} %pad_maximum_fusion.2), channel_id=1, source_target_pairs={{0,96},{32,0},{64,32},{96,64},{1,97},{33,1},{65,33},{97,65},{2,98}... | collective-permute-start | bytes 3145736 | tf_op jit(solution)/shard_map/ppermute | solution.py:358
  190.6 24.1 %collective-permute-start.7 = (bf16[128,4096]{1,0:T(8,128)(2,1)}, bf16[128,4096]{1,0:T(8,128)(2,1)}, u32[]{:S(2)}, u32[]{:S(2)}) collective-permute-start(bf16[128,4096]{1,0:T(8,128)(2,1)} %pad_maximum_fusion.1), channel_id=1, source_target_pairs={{0,32},{32,64},{64,96},{96,0},{1,33},{33,65},{65,97},{97,1},{2,34}... | collective-permute-start | bytes 3145736 | tf_op jit(solution)/shard_map/ppermute | solution.py:358
  217.2 7.9 %collective-permute-start.13 = (bf16[16,4096]{1,0:T(8,128)(2,1)S(1)}, bf16[16,4096]{1,0:T(8,128)(2,1)S(1)}, u32[]{:S(2)}, u32[]{:S(2)}) collective-permute-start(bf16[16,4096]{1,0:T(8,128)(2,1)S(1)} %get-tuple-element.117), channel_id=1, source_target_pairs={{0,32},{32,64},{64,96},{96,0},{1,33},{33,65},{65,97},{97,1},{2,34}... | collective-permute-start | bytes 393224 | tf_op jit(solution)/shard_map/ppermute | solution.py:346
  217.2 7.8 %collective-permute-start.14 = (bf16[16,4096]{1,0:T(8,128)(2,1)S(1)}, bf16[16,4096]{1,0:T(8,128)(2,1)S(1)}, u32[]{:S(2)}, u32[]{:S(2)}) collective-permute-start(bf16[16,4096]{1,0:T(8,128)(2,1)S(1)} %get-tuple-element.116), channel_id=1, source_target_pairs={{0,96},{32,0},{64,32},{96,64},{1,97},{33,1},{65,33},{97,65},{2,98}... | collective-permute-start | bytes 393224 | tf_op jit(solution)/shard_map/ppermute | solution.py:346
  222.3 5.1 %collective-permute-start.11 = (bf16[16,4096]{1,0:T(8,128)(2,1)S(1)}, bf16[16,4096]{1,0:T(8,128)(2,1)S(1)}, u32[]{:S(2)}, u32[]{:S(2)}) collective-permute-start(bf16[16,4096]{1,0:T(8,128)(2,1)S(1)} %get-tuple-element.123), channel_id=1, source_target_pairs={{0,8},{8,16},{16,24},{24,0},{1,9},{9,17},{17,25},{25,1},{2,10},{10... | collective-permute-start | bytes 393224 | tf_op jit(solution)/shard_map/ppermute | solution.py:346
  222.4 5.0 %collective-permute-start.12 = (bf16[16,4096]{1,0:T(8,128)(2,1)S(1)}, bf16[16,4096]{1,0:T(8,128)(2,1)S(1)}, u32[]{:S(2)}, u32[]{:S(2)}) collective-permute-start(bf16[16,4096]{1,0:T(8,128)(2,1)S(1)} %get-tuple-element.122), channel_id=1, source_target_pairs={{0,24},{8,0},{16,8},{24,16},{1,25},{9,1},{17,9},{25,17},{2,26},{10... | collective-permute-start | bytes 393224 | tf_op jit(solution)/shard_map/ppermute | solution.py:346
  227.5 5.3 %collective-permute-start.18 = (bf16[32,4096]{1,0:T(8,128)(2,1)S(1)}, bf16[32,4096]{1,0:T(8,128)(2,1)S(1)}, u32[]{:S(2)}, u32[]{:S(2)}) collective-permute-start(bf16[32,4096]{1,0:T(8,128)(2,1)S(1)} %pad_maximum_fusion.10), channel_id=1, source_target_pairs={{0,96},{32,0},{64,32},{96,64},{1,97},{33,1},{65,33},{97,65},{2,98}... | collective-permute-start | bytes 786440 | tf_op jit(solution)/shard_map/ppermute | solution.py:358
  227.9 6.6 %collective-permute-start.17 = (bf16[32,4096]{1,0:T(8,128)(2,1)S(1)}, bf16[32,4096]{1,0:T(8,128)(2,1)}, u32[]{:S(2)}, u32[]{:S(2)}) collective-permute-start(bf16[32,4096]{1,0:T(8,128)(2,1)S(1)} %pad_maximum_fusion.9), channel_id=1, source_target_pairs={{0,32},{32,64},{64,96},{96,0},{1,33},{33,65},{65,97},{97,1},{2,34}... | collective-permute-start | bytes 786440 | tf_op jit(solution)/shard_map/ppermute | solution.py:358
  229.2 6.1 %collective-permute-start.16 = (bf16[32,4096]{1,0:T(8,128)(2,1)S(1)}, bf16[32,4096]{1,0:T(8,128)(2,1)}, u32[]{:S(2)}, u32[]{:S(2)}) collective-permute-start(bf16[32,4096]{1,0:T(8,128)(2,1)S(1)} %pad_maximum_fusion.8), channel_id=1, source_target_pairs={{0,24},{8,0},{16,8},{24,16},{1,25},{9,1},{17,9},{25,17},{2,26},{10... | collective-permute-start | bytes 786440 | tf_op jit(solution)/shard_map/ppermute | solution.py:358
  232.0 6.9 %collective-permute-start.15 = (bf16[32,4096]{1,0:T(8,128)(2,1)S(1)}, bf16[32,4096]{1,0:T(8,128)(2,1)}, u32[]{:S(2)}, u32[]{:S(2)}) collective-permute-start(bf16[32,4096]{1,0:T(8,128)(2,1)S(1)} %pad_maximum_fusion.7), channel_id=1, source_target_pairs={{0,8},{8,16},{16,24},{24,0},{1,9},{9,17},{17,25},{25,1},{2,10},{10... | collective-permute-start | bytes 786440 | tf_op jit(solution)/shard_map/ppermute | solution.py:358
  241.1 7.9 %collective-permute-start.19 = (bf16[2,16,4096]{2,1,0:T(8,128)(2,1)S(1)}, bf16[2,16,4096]{2,1,0:T(8,128)(2,1)S(1)}, u32[]{:S(2)}, u32[]{:S(2)}) collective-permute-start(bf16[2,16,4096]{2,1,0:T(8,128)(2,1)S(1)} %get-tuple-element.129), channel_id=1, source_target_pairs={{0,4},{4,0},{1,5},{5,1},{2,6},{6,2},{3,7},{7,3},{8,12},{12,8},{9,1... | collective-permute-start | bytes 786440 | tf_op jit(solution)/shard_map/ppermute | solution.py:495
  (22 other events, 167.9 us)
Sparse Core Ops, SparseCore 0:
  10.8 76.2 all-gather.5
  107.8 47.2 all-gather.7
  157.7 31.3 all-gather.9

commit v2 on v1

--- a/solution.py
+++ b/solution.py
@@ -43,7 +43,7 @@
 
 
 def project_kernel(
-    rel, choose, x, dy, tall_w, wide_w, pre, coef, own, acc_x, acc_dy
+    rel, choose, x0, x1, x2, x3, dy0, dy1, dy2, dy3, tall_w, wide_w, pre, coef, own, acc_x, acc_dy
 ):
     j = pl.program_id(0)
 
@@ -52,7 +52,8 @@
         acc_x[...] = jnp.zeros_like(acc_x)
         acc_dy[...] = jnp.zeros_like(acc_dy)
 
-    xv, dv = x[...], dy[...]
+    xv = jnp.concatenate([r[...] for r in (x0, x1, x2, x3)], axis=0)
+    dv = jnp.concatenate([r[...] for r in (dy0, dy1, dy2, dy3)], axis=0)
     acc_x[:, : 2 * LANES] += dot(xv, tall_w[...])
     acc_x[:, 2 * LANES :] += dot_nt(xv, wide_w[2 * LANES :, :])
     acc_dy[...] += dot_nt(dv, wide_w[: 2 * LANES, :])
@@ -89,8 +90,8 @@
         in_specs=[
             pl.BlockSpec((rows, 1), lambda j: (0, 0)),
             pl.BlockSpec((cap, rows), lambda j: (0, 0)),
-            pl.BlockSpec((rows, width), lambda j: (0, j)),
-            pl.BlockSpec((rows, width), lambda j: (0, j + steps)),
+            *(pl.BlockSpec((rows // 4, width), lambda j, k=k: (k, j)) for k in range(4)),
+            *(pl.BlockSpec((rows // 4, width), lambda j, k=k: (k, j + steps)) for k in range(4)),
             pl.BlockSpec((width, tall_w.shape[1]), lambda j: (j, 0)),
             pl.BlockSpec((wide_w.shape[0], width), lambda j: (0, j)),
         ],
@@ -105,9 +106,9 @@
             jax.ShapeDtypeStruct((2 * cap, d), BF),
         ],
         scratch_shapes=[pltpu.VMEM((rows, 4 * LANES), F32), pltpu.VMEM((rows, 2 * LANES), F32)],
-        compiler_params=params(32),
+        compiler_params=params(56),
         name="project",
-    )(rel, choose, both, both, tall_w, wide_w)
+    )(rel, choose, *([both] * 8), tall_w, wide_w)
 
 
 def hidden_kernel(tenant, pos, pos_row, table, pre, b_g, b_u, a_d, values, placed, partial):
@@ -189,12 +190,12 @@
             jax.ShapeDtypeStruct((spots, LANES), BF),
         ],
         scratch_shapes=[pltpu.VMEM((rows, LANES), BF)],
-        compiler_params=params(40),
+        compiler_params=params(56),
         name="hidden_stage",
     )(tenant, pos, pos_row, table, pre, b_g, b_u, a_d)
 
 
-def left_kernel(rel, choose_t, low, order_m, order_i, values, left):
+def left_kernel(rel, choose_t, low, order_m, order_i, values, left, packed):
     rows = rel.shape[0]
     mine = rel[...] == (iota((rows, LANES), 1) >> 4)
     back = dot(choose_t[...], low[...]).astype(BF)
@@ -205,6 +206,9 @@
     for_input = jnp.concatenate(
         [values[:, LANES : 3 * LANES], spread(RANK, 1.0), spread(2 * RANK, 1.0)], axis=1
     )
+    packed[:rows, :] = values[...]
+    packed[rows:, :] = jnp.zeros((packed.shape[0] - rows, packed.shape[1]), BF)
+    packed[rows:, :LANES] = low[...]
     at = iota((rows, rows), 1)
     left[:, : 2 * LANES] = dot((order_m[...] == at).astype(BF), for_mixed).astype(BF)
     left[:, 2 * LANES :] = dot((order_i[...] == at).astype(BF), for_input).astype(BF)
@@ -214,8 +218,11 @@
     rows = rel.shape[0]
     return pl.pallas_call(
         left_kernel,
-        out_shape=jax.ShapeDtypeStruct((rows, 6 * LANES), BF),
-        compiler_params=params(40),
+        out_shape=[
+            jax.ShapeDtypeStruct((rows, 6 * LANES), BF),
+            jax.ShapeDtypeStruct((rows + low.shape[0], values.shape[1]), BF),
+        ],
+        compiler_params=params(56),
         name="left_stage",
     )(rel, choose_t, low, order_m, order_i, values)
 
@@ -265,7 +272,7 @@
             out_specs=[pl.BlockSpec((k, width), lambda j, c: (0, j)) for k in counts],
         ),
         out_shape=[jax.ShapeDtypeStruct((k, half), BF) for k in counts],
-        compiler_params=params(40),
+        compiler_params=params(56),
         name="products",
     )(core, left, other, tall_w, wide_w, near, side)
 
@@ -298,7 +305,7 @@
     return pl.pallas_call(
         tenant_kernel,
         out_shape=[shape] * 3,
-        compiler_params=params(40),
+        compiler_params=params(56),
         name="tenant_gradients",
     )(rel_tenant, values)
 
@@ -328,7 +335,7 @@
         ],
         out_specs=[spec] * 3,
         out_shape=[jax.ShapeDtypeStruct((n, d), F32)] * 3,
-        compiler_params=params(32),
+        compiler_params=params(56),
         name="slot_gradients",
     )(weights, own)
 
@@ -456,10 +463,9 @@
     terms = placed[:, : 3 * RANK].reshape(blk_count, cap, 3 * RANK)
     terms = lax.all_to_all(terms, BLK, split_axis=0, concat_axis=0, tiled=True)
     low = jnp.sum(terms.astype(F32), axis=0).astype(BF)
-    low = jnp.pad(low, ((0, cap), (0, LANES - 3 * RANK)))
-    left = left_stage(rel, jnp.transpose(choose), low[:cap], order_m, order_i, values)
+    low = jnp.pad(low, ((0, 0), (0, LANES - 3 * RANK)))
+    left, packed = left_stage(rel, jnp.transpose(choose), low, order_m, order_i, values)
     other = lax.ppermute(left, "c", SWAP)
-    packed = jnp.concatenate([values, low.reshape(-1, 4 * LANES)], axis=0)
     left, other, packed, all_own = lax.optimization_barrier((left, other, packed, all_own))
     packed = lax.all_gather(packed, "y", axis=0)
     pieces = products(
@@ -468,8 +474,7 @@
     pieces = (pieces[:3], pieces[3:])
     sent = first_step(*pieces, ("x", "z"))
     moved = second_start(*pieces, ("x", "z"), sent)
-    low_all = packed[:, group_rows:, :].astype(F32)
-    low_all = low_all.reshape(grp_count, -1, LANES)[:, :cap, : 3 * RANK]
+    low_all = packed[:, group_rows:, : 3 * RANK].astype(F32)
     slots_dev = per_owner // grp_count
     wanted = grp * slots_dev + jnp.arange(slots_dev, dtype=jnp.int32)
     weights = jnp.where(

time: 258 us -> 258 us (level)
  Pallas kernels: 45.1 us -> 59.4 us
  local copies, waits for them, and re-layouts: 32.7 us -> 22 us
  waiting for transfers between devices: 101 us -> 96.3 us
    unnamed x48 -> x23, local copies, waits for them, and re-layouts: 25.3 us -> 8.2 us
    pallas_call x1, Pallas kernels: 9.05 us -> 12.2 us  [hidden_stage(): pl.pallas_call(hidden_kernel, grid=(rows // part,), in_specs=[pl.BlockSpe...]
    pallas_call x1, Pallas kernels: 14.1 us -> 16.9 us  [project(): pl.pallas_call(project_kernel, grid=(steps,), in_specs=[pl.BlockSpec((row...]
    pallas_call x1, Pallas kernels: 4.04 us -> 6.85 us  [slot_gradients(): pl.pallas_call(slot_kernel, grid=(d // width,), in_specs=[pl.BlockSpec(we...]
  transfers between devices with their start and end apart: 25 -> 25, of which waited for: 15 -> 16; matrix products, arithmetic and copies ran while one was open for 11% -> 14% of each run, Pallas kernels for 12% -> 17%
where the time goes in v2:
time: 258 us; the launch traced here: 256 us
  waiting for transfers between devices  96.3 us (37%)
  Pallas kernels  59.4 us (23%)
  starting transfers between devices  39 us (15%)
  other arithmetic  25.6 us (10%)
  local copies, waits for them, and re-layouts  22 us (9%)
  between operations  14.2 us (6%)
    all_gather x1, waiting for transfers between devices, local(): both = lax.all_gather(both, BLK, axis=0, tiled=True)  57.4 us
    pallas_call x1, Pallas kernels, project(): pl.pallas_call(project_kernel, grid=(steps,), in_specs=[pl.BlockSpec((row...  16.9 us
    ppermute x8, waiting for transfers between devices, second_start(): moved += [lax.ppermute(right, axis, UP), lax.ppermute(left, axis, DOWN)]  13.6 us
    pallas_call x1, Pallas kernels, products(): pl.pallas_call(product_kernel, grid_spec=pltpu.PrefetchScalarGridSpec(num...  12.7 us
    pallas_call x1, Pallas kernels, hidden_stage(): pl.pallas_call(hidden_kernel, grid=(rows // part,), in_specs=[pl.BlockSpe...  12.2 us
    ppermute x8, waiting for transfers between devices, first_step(): sent += [lax.ppermute(p[0], axis, UP), lax.ppermute(p[1], axis, DOWN)]  11.1 us
    ppermute x8, starting transfers between devices, first_step(): sent += [lax.ppermute(p[0], axis, UP), lax.ppermute(p[1], axis, DOWN)]  10.9 us
    convert_element_type x8, other arithmetic, add(): return total.astype(BF)  9.86 us
  transfers between devices with their start and end apart: 25, of which 16 were waited for; matrix products, arithmetic and copies ran while one was open for 14% of the time, Pallas kernels for 17%

profile of v2, /device:TPU:1, one launch (start us, length us, event | category | flops | bytes accessed | tf_op | source)
XLA Modules:
  0.0 256.5 jit_solution(1740316693872157040)
XLA Ops:
  9.2 4.1 %pad_maximum_fusion.wide_w = bf16[512,8192]{1,0:T(8,128)(2,1)S(1)} fusion(bf16[128,8192]{1,0:T(8,128)(2,1)} %bitcast.48, bf16[128,8192]{1,0:T(8,128)(2,1)} %bitcast.49, bf16[128,8192]{1,0:T(8,128)(2,1)} %bitcast.50, bf16[128,8192]{1,0:T(8,128)(2,1)} %param.17), kind=kLoop, calls=%fused_computation | loop fusion | flops 33554432 | bytes 16777216 | tf_op jit(solution)/shard_map/concatenate | solution.py:438
  13.3 2.4 constant_dynamic-slice_fusion.1
  15.7 2.4 copy-done
  29.7 57.4 %all-gather.6.cloned.1.call-done.x0.x1.x2.x3.dy0.dy1.dy2.dy3 = bf16[512,16384]{1,0:T(8,128)(2,1)} async-done(((bf16[16,16384]{1,0:T(8,128)(2,1)}), bf16[512,16384]{1,0:T(8,128)(2,1)}) %all-gather.6.cloned.1.call-update) | async-done | bytes 16777232 | tf_op jit(solution)/shard_map/all_gather | solution.py:452
  87.1 16.9 %project.1 = (f32[512,384]{1,0:T(8,128)}, bf16[32,128]{1,0:T(8,128)(2,1)}, bf16[64,8192]{1,0:T(8,128)(2,1)}) custom-call(s32[512,1]{1,0:T(8,128)} %copy.35.rel, bf16[32,512]{1,0:T(8,128)(2,1)} %copy.32.choose, bf16[512,16384]{1,0:T(8,128)(2,1)} %all-gather.6.cloned.1.call-done.x0.x1.x2.x3.dy0.dy1.dy2.dy3, ...), custom_call_target="tpu_custom_call" | custom-call | tf_op jit(solution)/shard_map/project/pallas_call | solution.py:87
  106.7 5.4 %all-to-all-start = ((bf16[32,2,768]{2,1,0:T(2,128)(2,1)}), bf16[32,2,768]{2,1,0:T(2,128)(2,1)S(1)}, u32[]{:S(2)}, u32[]{:S(2)}) async-start(bf16[32,2,768]{2,1,0:T(2,128)(2,1)} %reshape.483), calls=%async_computation | async-start | bytes 196608 | tf_op jit(solution)/shard_map/all_to_all | solution.py:458
  113.0 6.6 %all-to-all-done = bf16[32,2,768]{2,1,0:T(2,128)(2,1)S(1)} async-done(((bf16[32,2,768]{2,1,0:T(2,128)(2,1)}), bf16[32,2,768]{2,1,0:T(2,128)(2,1)S(1)}, u32[]{:S(2)}, u32[]{:S(2)}) %all-to-all-start) | async-done | bytes 98336 | tf_op jit(solution)/shard_map/all_to_all | solution.py:458
  120.5 12.2 %hidden_stage.1 = (bf16[512,512]{1,0:T(8,128)(2,1)}, bf16[1024,128]{1,0:T(8,128)(2,1)}) custom-call(s32[512,1]{1,0:T(8,128)} %copy.33.tenant, s32[512,1]{1,0:T(8,128)} %copy.34.pos, s32[1,512]{1,0:T(1,128)} %copy-done.6, bf16[1024,128]{1,0:T(8,128)(2,1)} %pad.8.table, f32[512,384]{1,0:T(8,128)} %get-tuple-element.62.pre, bf16[4096,128]{1,0:T(8,128)(2,1)} %bitcast.54, ...), custom_call_target="tpu_custom_call" | custom-call | tf_op jit(solution)/shard_map/hidden_stage/pallas_call | solution.py:171
  134.7 3.9 %all-to-all-start.1 = ((bf16[32,2,768]{2,1,0:T(2,128)(2,1)}), bf16[32,2,768]{2,1,0:T(2,128)(2,1)S(1)}, u32[]{:S(2)}, u32[]{:S(2)}) async-start(bf16[32,2,768]{2,1,0:T(2,128)(2,1)} %reshape.485), calls=%async_computation.1 | async-start | bytes 196608 | tf_op jit(solution)/shard_map/all_to_all | solution.py:464
  140.0 6.2 %all-to-all-done.1 = bf16[32,2,768]{2,1,0:T(2,128)(2,1)S(1)} async-done(((bf16[32,2,768]{2,1,0:T(2,128)(2,1)}), bf16[32,2,768]{2,1,0:T(2,128)(2,1)S(1)}, u32[]{:S(2)}, u32[]{:S(2)}) %all-to-all-start.1) | async-done | bytes 98336 | tf_op jit(solution)/shard_map/all_to_all | solution.py:464
  147.1 3.3 %left_stage.1 = (bf16[512,768]{1,0:T(8,128)(2,1)}, bf16[544,512]{1,0:T(8,128)(2,1)}) custom-call(s32[512,1]{1,0:T(8,128)} %copy.35.rel, bf16[512,32]{1,0:T(8,128)(2,1)} %get-tuple-element.135.choose_t, bf16[32,128]{1,0:T(8,128)(2,1)} %pad.9.low, s32[512,1]{1,0:T(8,128)} %get-tuple-element.139.order_m, s32[512,1]{1,0:T(8,128)} %get-tuple-element.138.order_i, ...), custom_call_target="tpu_custom_call" | custom-call | tf_op jit(solution)/shard_map/left_stage/pallas_call | solution.py:219
  153.8 12.7 %products.1 = (bf16[64,4096]{1,0:T(8,128)(2,1)}, bf16[64,4096]{1,0:T(8,128)(2,1)}, bf16[384,4096]{1,0:T(8,128)(2,1)}, bf16[64,4096]{1,0:T(8,128)(2,1)}, bf16[64,...) custom-call(s32[1]{0:T(128)} %bitcast.core, bf16[512,768]{1,0:T(8,128)(2,1)} %get-tuple-element.68.left, ...), custom_call_target="tpu_custom_call" | custom-call | tf_op jit(solution)/shard_map/products/pallas_call | solution.py:259
  169.6 2.4 collective-permute-start.6
  174.5 6.7 %collective-permute-done.3 = bf16[64,4096]{1,0:T(8,128)(2,1)S(1)} collective-permute-done((bf16[64,4096]{1,0:T(8,128)(2,1)}, bf16[64,4096]{1,0:T(8,128)(2,1)S(1)}, u32[]{:S(2)}, u32[]{:S(2)}) %collective-permute-start.3) | collective-permute-done | bytes 524320 | tf_op jit(solution)/shard_map/ppermute | solution.py:353
  184.8 2.5 collective-permute-start.10
  192.8 7.4 %tenant_gradients.1 = (f32[1024,128]{1,0:T(8,128)}, f32[1024,128]{1,0:T(8,128)}, f32[1024,128]{1,0:T(8,128)}) custom-call(s32[4,512]{1,0:T(4,128)} %broadcast_subtract_fusion.rel_tenant, bf16[4,544,512]{2,1,0:T(8,128)(2,1)} %bitcast.47), custom_call_target="tpu_custom_call" | custom-call | tf_op jit(solution)/shard_map/tenant_gradients/pallas_call | solution.py:305
  200.9 6.8 %slot_gradients.1 = (f32[32,8192]{1,0:T(8,128)}, f32[32,8192]{1,0:T(8,128)}, f32[32,8192]{1,0:T(8,128)}) custom-call(bf16[96,128]{1,0:T(8,128)(2,1)} %pad_maximum_fusion.10.weights, bf16[4,64,8192]{2,1,0:T(8,128)(2,1)} %bitcast.45), custom_call_target="tpu_custom_call" | custom-call | tf_op jit(solution)/shard_map/slot_gradients/pallas_call | solution.py:329
  207.9 3.2 %collective-permute-done.9 = bf16[128,4096]{1,0:T(8,128)(2,1)} collective-permute-done((bf16[128,4096]{1,0:T(8,128)(2,1)S(1)}, bf16[128,4096]{1,0:T(8,128)(2,1)}, u32[]{:S(2)}, u32[]{:S(2)}) %collective-permute-start.9) | collective-permute-done | bytes 1048608 | tf_op jit(solution)/shard_map/ppermute | solution.py:365
  211.7 2.8 %collective-permute-done.7 = bf16[128,4096]{1,0:T(8,128)(2,1)} collective-permute-done((bf16[128,4096]{1,0:T(8,128)(2,1)}, bf16[128,4096]{1,0:T(8,128)(2,1)}, u32[]{:S(2)}, u32[]{:S(2)}) %collective-permute-start.7) | collective-permute-done | bytes 1048608 | tf_op jit(solution)/shard_map/ppermute | solution.py:365
  217.0 2.7 %collective-permute-start.14 = (bf16[16,4096]{1,0:T(8,128)(2,1)S(1)}, bf16[16,4096]{1,0:T(8,128)(2,1)S(1)}, u32[]{:S(2)}, u32[]{:S(2)}) collective-permute-start(bf16[16,4096]{1,0:T(8,128)(2,1)S(1)} %get-tuple-element.120), channel_id=1, source_target_pairs={{0,96},{32,0},{64,32},{96,64},{1,97},{33,1},{65,33},{97,65},{2,98}... | collective-permute-start | bytes 393224 | tf_op jit(solution)/shard_map/ppermute | solution.py:353
  222.1 2.7 %collective-permute-start.12 = (bf16[16,4096]{1,0:T(8,128)(2,1)S(1)}, bf16[16,4096]{1,0:T(8,128)(2,1)S(1)}, u32[]{:S(2)}, u32[]{:S(2)}) collective-permute-start(bf16[16,4096]{1,0:T(8,128)(2,1)S(1)} %get-tuple-element.126), channel_id=1, source_target_pairs={{0,24},{8,0},{16,8},{24,16},{1,25},{9,1},{17,9},{25,17},{2,26},{10... | collective-permute-start | bytes 393224 | tf_op jit(solution)/shard_map/ppermute | solution.py:353
  228.9 2.7 %collective-permute-start.16 = (bf16[32,4096]{1,0:T(8,128)(2,1)S(1)}, bf16[32,4096]{1,0:T(8,128)(2,1)}, u32[]{:S(2)}, u32[]{:S(2)}) collective-permute-start(bf16[32,4096]{1,0:T(8,128)(2,1)S(1)} %pad_maximum_fusion.7), channel_id=1, source_target_pairs={{0,24},{8,0},{16,8},{24,16},{1,25},{9,1},{17,9},{25,17},{2,26},{10... | collective-permute-start | bytes 786440 | tf_op jit(solution)/shard_map/ppermute | solution.py:365
  235.0 3.6 %collective-permute-done.15 = bf16[32,4096]{1,0:T(8,128)(2,1)} collective-permute-done((bf16[32,4096]{1,0:T(8,128)(2,1)S(1)}, bf16[32,4096]{1,0:T(8,128)(2,1)}, u32[]{:S(2)}, u32[]{:S(2)}) %collective-permute-start.15) | collective-permute-done | bytes 262176 | tf_op jit(solution)/shard_map/ppermute | solution.py:365
  240.9 7.0 %collective-permute-start.19 = (bf16[2,16,4096]{2,1,0:T(8,128)(2,1)S(1)}, bf16[2,16,4096]{2,1,0:T(8,128)(2,1)S(1)}, u32[]{:S(2)}, u32[]{:S(2)}) collective-permute-start(bf16[2,16,4096]{2,1,0:T(8,128)(2,1)S(1)} %get-tuple-element.133), channel_id=1, source_target_pairs={{0,4},{4,0},{1,5},{5,1},{2,6},{6,2},{3,7},{7,3},{8,12},{12,8},{9,1... | collective-permute-start | bytes 786440 | tf_op jit(solution)/shard_map/ppermute | solution.py:500
  (122 shorter events, 58.3 us)
Async XLA Ops:
  7.2 79.9 %all-gather.6.cloned.1.call-start = ((), (), s32[]{:S(2)}) async-start(), calls=%async_computation.2 | async-start | bytes 17301504 | tf_op jit(solution)/shard_map/all_gather | solution.py:452
  9.1 143.8 %all-gather.8.cloned.1.call-start = ((), (), s32[]{:S(2)}) async-start(), calls=%async_computation.3 | async-start | bytes 5242880 | tf_op jit(solution)/shard_map/all_gather | solution.py:456
  18.1 11.6 %collective-permute-start = (bf16[512,4096]{1,0:T(8,128)(2,1)}, bf16[512,4096]{1,0:T(8,128)(2,1)}, u32[]{:S(2)}, u32[]{:S(2)}) collective-permute-start(bf16[512,4096]{1,0:T(8,128)(2,1)} %constant_dynamic-slice_fusion.1), channel_id=1, source_target_pairs={{0,4},{4,0},{1,5},{5,1},{2,6},{6,2},{3,7},{7,3},{8,12},{12,8},{9,1... | collective-permute-start | bytes 12582920 | tf_op jit(solution)/shard_map/ppermute | solution.py:440
  23.1 6.6 %collective-permute-start.1 = (bf16[4096,256]{1,0:T(8,128)(2,1)}, bf16[4096,256]{1,0:T(8,128)(2,1)S(1)}, u32[]{:S(2)}, u32[]{:S(2)}) collective-permute-start(bf16[4096,256]{1,0:T(8,128)(2,1)} %constant_dynamic-slice_fusion), channel_id=1, source_target_pairs={{0,4},{4,0},{1,5},{5,1},{2,6},{6,2},{3,7},{7,3},{8,12},{12,8},{9,1... | collective-permute-start | bytes 6291464 | tf_op jit(solution)/shard_map/ppermute | solution.py:441
  106.7 12.8 %all-to-all-start = ((bf16[32,2,768]{2,1,0:T(2,128)(2,1)}), bf16[32,2,768]{2,1,0:T(2,128)(2,1)S(1)}, u32[]{:S(2)}, u32[]{:S(2)}) async-start(bf16[32,2,768]{2,1,0:T(2,128)(2,1)} %reshape.483), calls=%async_computation | async-start | bytes 196608 | tf_op jit(solution)/shard_map/all_to_all | solution.py:458
  134.7 11.5 %all-to-all-start.1 = ((bf16[32,2,768]{2,1,0:T(2,128)(2,1)}), bf16[32,2,768]{2,1,0:T(2,128)(2,1)S(1)}, u32[]{:S(2)}, u32[]{:S(2)}) async-start(bf16[32,2,768]{2,1,0:T(2,128)(2,1)} %reshape.485), calls=%async_computation.1 | async-start | bytes 196608 | tf_op jit(solution)/shard_map/all_to_all | solution.py:464
  138.6 53.2 %all-gather.10.cloned.1.call-start = ((), (), s32[]{:S(2)}) async-start(), calls=%async_computation.4 | async-start | bytes 2785280 | tf_op jit(solution)/shard_map/all_gather | solution.py:470
  166.5 14.7 %collective-permute-start.3 = (bf16[64,4096]{1,0:T(8,128)(2,1)}, bf16[64,4096]{1,0:T(8,128)(2,1)S(1)}, u32[]{:S(2)}, u32[]{:S(2)}) collective-permute-start(bf16[64,4096]{1,0:T(8,128)(2,1)} %get-tuple-element.73), channel_id=1, source_target_pairs={{0,32},{32,64},{64,96},{96,0},{1,33},{33,65},{65,97},{97,1},{2,34}... | collective-permute-start | bytes 1572872 | tf_op jit(solution)/shard_map/ppermute | solution.py:353
  166.9 14.3 %collective-permute-start.4 = (bf16[64,4096]{1,0:T(8,128)(2,1)}, bf16[64,4096]{1,0:T(8,128)(2,1)S(1)}, u32[]{:S(2)}, u32[]{:S(2)}) collective-permute-start(bf16[64,4096]{1,0:T(8,128)(2,1)} %get-tuple-element.74), channel_id=1, source_target_pairs={{0,96},{32,0},{64,32},{96,64},{1,97},{33,1},{65,33},{97,65},{2,98}... | collective-permute-start | bytes 1572872 | tf_op jit(solution)/shard_map/ppermute | solution.py:353
  169.2 14.0 %collective-permute-start.5 = (bf16[64,4096]{1,0:T(8,128)(2,1)}, bf16[64,4096]{1,0:T(8,128)(2,1)S(1)}, u32[]{:S(2)}, u32[]{:S(2)}) collective-permute-start(bf16[64,4096]{1,0:T(8,128)(2,1)} %get-tuple-element.75), channel_id=1, source_target_pairs={{0,8},{8,16},{16,24},{24,0},{1,9},{9,17},{17,25},{25,1},{2,10},{10... | collective-permute-start | bytes 1572872 | tf_op jit(solution)/shard_map/ppermute | solution.py:353
  169.6 13.7 %collective-permute-start.6 = (bf16[64,4096]{1,0:T(8,128)(2,1)}, bf16[64,4096]{1,0:T(8,128)(2,1)S(1)}, u32[]{:S(2)}, u32[]{:S(2)}) collective-permute-start(bf16[64,4096]{1,0:T(8,128)(2,1)} %get-tuple-element.76), channel_id=1, source_target_pairs={{0,24},{8,0},{16,8},{24,16},{1,25},{9,1},{17,9},{25,17},{2,26},{10... | collective-permute-start | bytes 1572872 | tf_op jit(solution)/shard_map/ppermute | solution.py:353
  184.8 23.1 %collective-permute-start.10 = (bf16[128,4096]{1,0:T(8,128)(2,1)S(1)}, bf16[128,4096]{1,0:T(8,128)(2,1)}, u32[]{:S(2)}, u32[]{:S(2)}) collective-permute-start(bf16[128,4096]{1,0:T(8,128)(2,1)S(1)} %pad_maximum_fusion.4), channel_id=1, source_target_pairs={{0,24},{8,0},{16,8},{24,16},{1,25},{9,1},{17,9},{25,17},{2,26},{10... | collective-permute-start | bytes 3145736 | tf_op jit(solution)/shard_map/ppermute | solution.py:365
  187.3 23.7 %collective-permute-start.9 = (bf16[128,4096]{1,0:T(8,128)(2,1)S(1)}, bf16[128,4096]{1,0:T(8,128)(2,1)}, u32[]{:S(2)}, u32[]{:S(2)}) collective-permute-start(bf16[128,4096]{1,0:T(8,128)(2,1)S(1)} %pad_maximum_fusion.3), channel_id=1, source_target_pairs={{0,8},{8,16},{16,24},{24,0},{1,9},{9,17},{17,25},{25,1},{2,10},{10... | collective-permute-start | bytes 3145736 | tf_op jit(solution)/shard_map/ppermute | solution.py:365
  188.9 22.7 %collective-permute-start.8 = (bf16[128,4096]{1,0:T(8,128)(2,1)S(1)}, bf16[128,4096]{1,0:T(8,128)(2,1)}, u32[]{:S(2)}, u32[]{:S(2)}) collective-permute-start(bf16[128,4096]{1,0:T(8,128)(2,1)S(1)} %pad_maximum_fusion.2), channel_id=1, source_target_pairs={{0,96},{32,0},{64,32},{96,64},{1,97},{33,1},{65,33},{97,65},{2,98}... | collective-permute-start | bytes 3145736 | tf_op jit(solution)/shard_map/ppermute | solution.py:365
  190.7 23.9 %collective-permute-start.7 = (bf16[128,4096]{1,0:T(8,128)(2,1)}, bf16[128,4096]{1,0:T(8,128)(2,1)}, u32[]{:S(2)}, u32[]{:S(2)}) collective-permute-start(bf16[128,4096]{1,0:T(8,128)(2,1)} %pad_maximum_fusion.1), channel_id=1, source_target_pairs={{0,32},{32,64},{64,96},{96,0},{1,33},{33,65},{65,97},{97,1},{2,34}... | collective-permute-start | bytes 3145736 | tf_op jit(solution)/shard_map/ppermute | solution.py:365
  216.9 7.9 %collective-permute-start.13 = (bf16[16,4096]{1,0:T(8,128)(2,1)S(1)}, bf16[16,4096]{1,0:T(8,128)(2,1)S(1)}, u32[]{:S(2)}, u32[]{:S(2)}) collective-permute-start(bf16[16,4096]{1,0:T(8,128)(2,1)S(1)} %get-tuple-element.121), channel_id=1, source_target_pairs={{0,32},{32,64},{64,96},{96,0},{1,33},{33,65},{65,97},{97,1},{2,34}... | collective-permute-start | bytes 393224 | tf_op jit(solution)/shard_map/ppermute | solution.py:353
  217.0 7.8 %collective-permute-start.14 = (bf16[16,4096]{1,0:T(8,128)(2,1)S(1)}, bf16[16,4096]{1,0:T(8,128)(2,1)S(1)}, u32[]{:S(2)}, u32[]{:S(2)}) collective-permute-start(bf16[16,4096]{1,0:T(8,128)(2,1)S(1)} %get-tuple-element.120), channel_id=1, source_target_pairs={{0,96},{32,0},{64,32},{96,64},{1,97},{33,1},{65,33},{97,65},{2,98}... | collective-permute-start | bytes 393224 | tf_op jit(solution)/shard_map/ppermute | solution.py:353
  222.0 5.1 %collective-permute-start.11 = (bf16[16,4096]{1,0:T(8,128)(2,1)S(1)}, bf16[16,4096]{1,0:T(8,128)(2,1)S(1)}, u32[]{:S(2)}, u32[]{:S(2)}) collective-permute-start(bf16[16,4096]{1,0:T(8,128)(2,1)S(1)} %get-tuple-element.127), channel_id=1, source_target_pairs={{0,8},{8,16},{16,24},{24,0},{1,9},{9,17},{17,25},{25,1},{2,10},{10... | collective-permute-start | bytes 393224 | tf_op jit(solution)/shard_map/ppermute | solution.py:353
  222.1 5.0 %collective-permute-start.12 = (bf16[16,4096]{1,0:T(8,128)(2,1)S(1)}, bf16[16,4096]{1,0:T(8,128)(2,1)S(1)}, u32[]{:S(2)}, u32[]{:S(2)}) collective-permute-start(bf16[16,4096]{1,0:T(8,128)(2,1)S(1)} %get-tuple-element.126), channel_id=1, source_target_pairs={{0,24},{8,0},{16,8},{24,16},{1,25},{9,1},{17,9},{25,17},{2,26},{10... | collective-permute-start | bytes 393224 | tf_op jit(solution)/shard_map/ppermute | solution.py:353
  227.2 5.3 %collective-permute-start.18 = (bf16[32,4096]{1,0:T(8,128)(2,1)S(1)}, bf16[32,4096]{1,0:T(8,128)(2,1)S(1)}, u32[]{:S(2)}, u32[]{:S(2)}) collective-permute-start(bf16[32,4096]{1,0:T(8,128)(2,1)S(1)} %pad_maximum_fusion.9), channel_id=1, source_target_pairs={{0,96},{32,0},{64,32},{96,64},{1,97},{33,1},{65,33},{97,65},{2,98}... | collective-permute-start | bytes 786440 | tf_op jit(solution)/shard_map/ppermute | solution.py:365
  227.3 6.6 %collective-permute-start.17 = (bf16[32,4096]{1,0:T(8,128)(2,1)S(1)}, bf16[32,4096]{1,0:T(8,128)(2,1)}, u32[]{:S(2)}, u32[]{:S(2)}) collective-permute-start(bf16[32,4096]{1,0:T(8,128)(2,1)S(1)} %pad_maximum_fusion.8), channel_id=1, source_target_pairs={{0,32},{32,64},{64,96},{96,0},{1,33},{33,65},{65,97},{97,1},{2,34}... | collective-permute-start | bytes 786440 | tf_op jit(solution)/shard_map/ppermute | solution.py:365
  228.9 6.1 %collective-permute-start.16 = (bf16[32,4096]{1,0:T(8,128)(2,1)S(1)}, bf16[32,4096]{1,0:T(8,128)(2,1)}, u32[]{:S(2)}, u32[]{:S(2)}) collective-permute-start(bf16[32,4096]{1,0:T(8,128)(2,1)S(1)} %pad_maximum_fusion.7), channel_id=1, source_target_pairs={{0,24},{8,0},{16,8},{24,16},{1,25},{9,1},{17,9},{25,17},{2,26},{10... | collective-permute-start | bytes 786440 | tf_op jit(solution)/shard_map/ppermute | solution.py:365
  231.7 6.9 %collective-permute-start.15 = (bf16[32,4096]{1,0:T(8,128)(2,1)S(1)}, bf16[32,4096]{1,0:T(8,128)(2,1)}, u32[]{:S(2)}, u32[]{:S(2)}) collective-permute-start(bf16[32,4096]{1,0:T(8,128)(2,1)S(1)} %pad_maximum_fusion.6), channel_id=1, source_target_pairs={{0,8},{8,16},{16,24},{24,0},{1,9},{9,17},{17,25},{25,1},{2,10},{10... | collective-permute-start | bytes 786440 | tf_op jit(solution)/shard_map/ppermute | solution.py:365
  240.9 8.2 %collective-permute-start.19 = (bf16[2,16,4096]{2,1,0:T(8,128)(2,1)S(1)}, bf16[2,16,4096]{2,1,0:T(8,128)(2,1)S(1)}, u32[]{:S(2)}, u32[]{:S(2)}) collective-permute-start(bf16[2,16,4096]{2,1,0:T(8,128)(2,1)S(1)} %get-tuple-element.133), channel_id=1, source_target_pairs={{0,4},{4,0},{1,5},{5,1},{2,6},{6,2},{3,7},{7,3},{8,12},{12,8},{9,1... | collective-permute-start | bytes 786440 | tf_op jit(solution)/shard_map/ppermute | solution.py:500
  (10 other events, 117.8 us)
Sparse Core Ops, SparseCore 0:
  10.8 76.2 all-gather.5
  104.2 47.2 all-gather.7
  153.1 32.2 all-gather.9

commit v3 on v2

--- a/solution.py
+++ b/solution.py
@@ -82,7 +82,7 @@
 def project(rel, choose, both, tall_w, wide_w):
     rows, d = both.shape[0], both.shape[1] // 2
     cap = choose.shape[0]
-    width = 1024
+    width = 2048
     steps = d // width
     return pl.pallas_call(
         project_kernel,
@@ -165,7 +165,7 @@
 
 def hidden_stage(tenant, pos, pos_row, table, pre, b_g, b_u, a_d):
     rows = pre.shape[0]
-    part = 256
+    part = 512
     whole = lambda a: pl.BlockSpec(a.shape, lambda j: (0, 0))
     spots = table.shape[0]
     return pl.pallas_call(

time: 258 us -> 256 us (level)
  no operation moved by 1% of the time
where the time goes in v3:
time: 256 us; the launch traced here: 255 us
  waiting for transfers between devices  96.3 us (38%)
  Pallas kernels  58.2 us (23%)
  starting transfers between devices  39.1 us (15%)
  other arithmetic  25.6 us (10%)
  local copies, waits for them, and re-layouts  22 us (9%)
  between operations  14.2 us (6%)
    all_gather x1, waiting for transfers between devices, local(): both = lax.all_gather(both, BLK, axis=0, tiled=True)  57.4 us
    pallas_call x1, Pallas kernels, project(): pl.pallas_call(project_kernel, grid=(steps,), in_specs=[pl.BlockSpec((row...  15.8 us
    ppermute x8, waiting for transfers between devices, second_start(): moved += [lax.ppermute(right, axis, UP), lax.ppermute(left, axis, DOWN)]  13.6 us
    pallas_call x1, Pallas kernels, products(): pl.pallas_call(product_kernel, grid_spec=pltpu.PrefetchScalarGridSpec(num...  12.7 us
    pallas_call x1, Pallas kernels, hidden_stage(): pl.pallas_call(hidden_kernel, grid=(rows // part,), in_specs=[pl.BlockSpe...  12.1 us
    ppermute x8, starting transfers between devices, first_step(): sent += [lax.ppermute(p[0], axis, UP), lax.ppermute(p[1], axis, DOWN)]  11.2 us
    ppermute x8, waiting for transfers between devices, first_step(): sent += [lax.ppermute(p[0], axis, UP), lax.ppermute(p[1], axis, DOWN)]  11.1 us
    convert_element_type x8, other arithmetic, add(): return total.astype(BF)  9.86 us
  transfers between devices with their start and end apart: 25, of which 16 were waited for; matrix products, arithmetic and copies ran while one was open for 14% of the time, Pallas kernels for 17%

profile of v3, /device:TPU:1, one launch (start us, length us, event | category | flops | bytes accessed | tf_op | source)
XLA Modules:
  0.0 255.3 jit_solution(13956030267725037272)
XLA Ops:
  9.2 4.1 %pad_maximum_fusion.wide_w = bf16[512,8192]{1,0:T(8,128)(2,1)S(1)} fusion(bf16[128,8192]{1,0:T(8,128)(2,1)} %bitcast.48, bf16[128,8192]{1,0:T(8,128)(2,1)} %bitcast.49, bf16[128,8192]{1,0:T(8,128)(2,1)} %bitcast.50, bf16[128,8192]{1,0:T(8,128)(2,1)} %param.17), kind=kLoop, calls=%fused_computation | loop fusion | flops 33554432 | bytes 16777216 | tf_op jit(solution)/shard_map/concatenate | solution.py:438
  13.3 2.4 constant_dynamic-slice_fusion.1
  15.7 2.4 copy-done
  29.7 57.4 %all-gather.6.cloned.1.call-done.x0.x1.x2.x3.dy0.dy1.dy2.dy3 = bf16[512,16384]{1,0:T(8,128)(2,1)} async-done(((bf16[16,16384]{1,0:T(8,128)(2,1)}), bf16[512,16384]{1,0:T(8,128)(2,1)}) %all-gather.6.cloned.1.call-update) | async-done | bytes 16777232 | tf_op jit(solution)/shard_map/all_gather | solution.py:452
  87.1 15.8 %project.1 = (f32[512,384]{1,0:T(8,128)}, bf16[32,128]{1,0:T(8,128)(2,1)}, bf16[64,8192]{1,0:T(8,128)(2,1)}) custom-call(s32[512,1]{1,0:T(8,128)} %copy.35.rel, bf16[32,512]{1,0:T(8,128)(2,1)} %copy.32.choose, bf16[512,16384]{1,0:T(8,128)(2,1)} %all-gather.6.cloned.1.call-done.x0.x1.x2.x3.dy0.dy1.dy2.dy3, ...), custom_call_target="tpu_custom_call" | custom-call | tf_op jit(solution)/shard_map/project/pallas_call | solution.py:87
  105.6 5.4 %all-to-all-start = ((bf16[32,2,768]{2,1,0:T(2,128)(2,1)}), bf16[32,2,768]{2,1,0:T(2,128)(2,1)S(1)}, u32[]{:S(2)}, u32[]{:S(2)}) async-start(bf16[32,2,768]{2,1,0:T(2,128)(2,1)} %reshape.483), calls=%async_computation | async-start | bytes 196608 | tf_op jit(solution)/shard_map/all_to_all | solution.py:458
  111.9 6.6 %all-to-all-done = bf16[32,2,768]{2,1,0:T(2,128)(2,1)S(1)} async-done(((bf16[32,2,768]{2,1,0:T(2,128)(2,1)}), bf16[32,2,768]{2,1,0:T(2,128)(2,1)S(1)}, u32[]{:S(2)}, u32[]{:S(2)}) %all-to-all-start) | async-done | bytes 98336 | tf_op jit(solution)/shard_map/all_to_all | solution.py:458
  119.4 12.1 %hidden_stage.1 = (bf16[512,512]{1,0:T(8,128)(2,1)}, bf16[1024,128]{1,0:T(8,128)(2,1)}) custom-call(s32[512,1]{1,0:T(8,128)} %copy.33.tenant, s32[512,1]{1,0:T(8,128)} %copy.34.pos, s32[1,512]{1,0:T(1,128)} %copy-done.6, bf16[1024,128]{1,0:T(8,128)(2,1)} %pad.8.table, f32[512,384]{1,0:T(8,128)} %get-tuple-element.62.pre, bf16[4096,128]{1,0:T(8,128)(2,1)} %bitcast.54, ...), custom_call_target="tpu_custom_call" | custom-call | tf_op jit(solution)/shard_map/hidden_stage/pallas_call | solution.py:171
  133.5 3.9 %all-to-all-start.1 = ((bf16[32,2,768]{2,1,0:T(2,128)(2,1)}), bf16[32,2,768]{2,1,0:T(2,128)(2,1)S(1)}, u32[]{:S(2)}, u32[]{:S(2)}) async-start(bf16[32,2,768]{2,1,0:T(2,128)(2,1)} %reshape.485), calls=%async_computation.1 | async-start | bytes 196608 | tf_op jit(solution)/shard_map/all_to_all | solution.py:464
  138.8 6.2 %all-to-all-done.1 = bf16[32,2,768]{2,1,0:T(2,128)(2,1)S(1)} async-done(((bf16[32,2,768]{2,1,0:T(2,128)(2,1)}), bf16[32,2,768]{2,1,0:T(2,128)(2,1)S(1)}, u32[]{:S(2)}, u32[]{:S(2)}) %all-to-all-start.1) | async-done | bytes 98336 | tf_op jit(solution)/shard_map/all_to_all | solution.py:464
  145.9 3.3 %left_stage.1 = (bf16[512,768]{1,0:T(8,128)(2,1)}, bf16[544,512]{1,0:T(8,128)(2,1)}) custom-call(s32[512,1]{1,0:T(8,128)} %copy.35.rel, bf16[512,32]{1,0:T(8,128)(2,1)} %get-tuple-element.135.choose_t, bf16[32,128]{1,0:T(8,128)(2,1)} %pad.9.low, s32[512,1]{1,0:T(8,128)} %get-tuple-element.139.order_m, s32[512,1]{1,0:T(8,128)} %get-tuple-element.138.order_i, ...), custom_call_target="tpu_custom_call" | custom-call | tf_op jit(solution)/shard_map/left_stage/pallas_call | solution.py:219
  152.6 12.7 %products.1 = (bf16[64,4096]{1,0:T(8,128)(2,1)}, bf16[64,4096]{1,0:T(8,128)(2,1)}, bf16[384,4096]{1,0:T(8,128)(2,1)}, bf16[64,4096]{1,0:T(8,128)(2,1)}, bf16[64,...) custom-call(s32[1]{0:T(128)} %bitcast.core, bf16[512,768]{1,0:T(8,128)(2,1)} %get-tuple-element.68.left, ...), custom_call_target="tpu_custom_call" | custom-call | tf_op jit(solution)/shard_map/products/pallas_call | solution.py:259
  168.4 2.4 collective-permute-start.6
  173.3 6.7 %collective-permute-done.3 = bf16[64,4096]{1,0:T(8,128)(2,1)S(1)} collective-permute-done((bf16[64,4096]{1,0:T(8,128)(2,1)}, bf16[64,4096]{1,0:T(8,128)(2,1)S(1)}, u32[]{:S(2)}, u32[]{:S(2)}) %collective-permute-start.3) | collective-permute-done | bytes 524320 | tf_op jit(solution)/shard_map/ppermute | solution.py:353
  183.6 2.5 collective-permute-start.10
  191.4 7.4 %tenant_gradients.1 = (f32[1024,128]{1,0:T(8,128)}, f32[1024,128]{1,0:T(8,128)}, f32[1024,128]{1,0:T(8,128)}) custom-call(s32[4,512]{1,0:T(4,128)} %broadcast_subtract_fusion.rel_tenant, bf16[4,544,512]{2,1,0:T(8,128)(2,1)} %bitcast.47), custom_call_target="tpu_custom_call" | custom-call | tf_op jit(solution)/shard_map/tenant_gradients/pallas_call | solution.py:305
  199.5 6.8 %slot_gradients.1 = (f32[32,8192]{1,0:T(8,128)}, f32[32,8192]{1,0:T(8,128)}, f32[32,8192]{1,0:T(8,128)}) custom-call(bf16[96,128]{1,0:T(8,128)(2,1)} %pad_maximum_fusion.10.weights, bf16[4,64,8192]{2,1,0:T(8,128)(2,1)} %bitcast.45), custom_call_target="tpu_custom_call" | custom-call | tf_op jit(solution)/shard_map/slot_gradients/pallas_call | solution.py:329
  206.7 3.2 %collective-permute-done.9 = bf16[128,4096]{1,0:T(8,128)(2,1)} collective-permute-done((bf16[128,4096]{1,0:T(8,128)(2,1)S(1)}, bf16[128,4096]{1,0:T(8,128)(2,1)}, u32[]{:S(2)}, u32[]{:S(2)}) %collective-permute-start.9) | collective-permute-done | bytes 1048608 | tf_op jit(solution)/shard_map/ppermute | solution.py:365
  210.3 2.8 %collective-permute-done.7 = bf16[128,4096]{1,0:T(8,128)(2,1)} collective-permute-done((bf16[128,4096]{1,0:T(8,128)(2,1)}, bf16[128,4096]{1,0:T(8,128)(2,1)}, u32[]{:S(2)}, u32[]{:S(2)}) %collective-permute-start.7) | collective-permute-done | bytes 1048608 | tf_op jit(solution)/shard_map/ppermute | solution.py:365
  215.6 2.7 %collective-permute-start.14 = (bf16[16,4096]{1,0:T(8,128)(2,1)S(1)}, bf16[16,4096]{1,0:T(8,128)(2,1)S(1)}, u32[]{:S(2)}, u32[]{:S(2)}) collective-permute-start(bf16[16,4096]{1,0:T(8,128)(2,1)S(1)} %get-tuple-element.120), channel_id=1, source_target_pairs={{0,96},{32,0},{64,32},{96,64},{1,97},{33,1},{65,33},{97,65},{2,98}... | collective-permute-start | bytes 393224 | tf_op jit(solution)/shard_map/ppermute | solution.py:353
  220.9 2.7 %collective-permute-start.12 = (bf16[16,4096]{1,0:T(8,128)(2,1)S(1)}, bf16[16,4096]{1,0:T(8,128)(2,1)S(1)}, u32[]{:S(2)}, u32[]{:S(2)}) collective-permute-start(bf16[16,4096]{1,0:T(8,128)(2,1)S(1)} %get-tuple-element.126), channel_id=1, source_target_pairs={{0,24},{8,0},{16,8},{24,16},{1,25},{9,1},{17,9},{25,17},{2,26},{10... | collective-permute-start | bytes 393224 | tf_op jit(solution)/shard_map/ppermute | solution.py:353
  227.8 2.7 %collective-permute-start.16 = (bf16[32,4096]{1,0:T(8,128)(2,1)S(1)}, bf16[32,4096]{1,0:T(8,128)(2,1)}, u32[]{:S(2)}, u32[]{:S(2)}) collective-permute-start(bf16[32,4096]{1,0:T(8,128)(2,1)S(1)} %pad_maximum_fusion.7), channel_id=1, source_target_pairs={{0,24},{8,0},{16,8},{24,16},{1,25},{9,1},{17,9},{25,17},{2,26},{10... | collective-permute-start | bytes 786440 | tf_op jit(solution)/shard_map/ppermute | solution.py:365
  233.8 3.6 %collective-permute-done.15 = bf16[32,4096]{1,0:T(8,128)(2,1)} collective-permute-done((bf16[32,4096]{1,0:T(8,128)(2,1)S(1)}, bf16[32,4096]{1,0:T(8,128)(2,1)}, u32[]{:S(2)}, u32[]{:S(2)}) %collective-permute-start.15) | collective-permute-done | bytes 262176 | tf_op jit(solution)/shard_map/ppermute | solution.py:365
  239.7 7.0 %collective-permute-start.19 = (bf16[2,16,4096]{2,1,0:T(8,128)(2,1)S(1)}, bf16[2,16,4096]{2,1,0:T(8,128)(2,1)S(1)}, u32[]{:S(2)}, u32[]{:S(2)}) collective-permute-start(bf16[2,16,4096]{2,1,0:T(8,128)(2,1)S(1)} %get-tuple-element.133), channel_id=1, source_target_pairs={{0,4},{4,0},{1,5},{5,1},{2,6},{6,2},{3,7},{7,3},{8,12},{12,8},{9,1... | collective-permute-start | bytes 786440 | tf_op jit(solution)/shard_map/ppermute | solution.py:500
  (122 shorter events, 58.3 us)
Async XLA Ops:
  7.2 79.9 %all-gather.6.cloned.1.call-start = ((), (), s32[]{:S(2)}) async-start(), calls=%async_computation.2 | async-start | bytes 17301504 | tf_op jit(solution)/shard_map/all_gather | solution.py:452
  9.1 142.7 %all-gather.8.cloned.1.call-start = ((), (), s32[]{:S(2)}) async-start(), calls=%async_computation.3 | async-start | bytes 5242880 | tf_op jit(solution)/shard_map/all_gather | solution.py:456
  18.1 11.6 %collective-permute-start = (bf16[512,4096]{1,0:T(8,128)(2,1)}, bf16[512,4096]{1,0:T(8,128)(2,1)}, u32[]{:S(2)}, u32[]{:S(2)}) collective-permute-start(bf16[512,4096]{1,0:T(8,128)(2,1)} %constant_dynamic-slice_fusion.1), channel_id=1, source_target_pairs={{0,4},{4,0},{1,5},{5,1},{2,6},{6,2},{3,7},{7,3},{8,12},{12,8},{9,1... | collective-permute-start | bytes 12582920 | tf_op jit(solution)/shard_map/ppermute | solution.py:440
  23.1 6.6 %collective-permute-start.1 = (bf16[4096,256]{1,0:T(8,128)(2,1)}, bf16[4096,256]{1,0:T(8,128)(2,1)S(1)}, u32[]{:S(2)}, u32[]{:S(2)}) collective-permute-start(bf16[4096,256]{1,0:T(8,128)(2,1)} %constant_dynamic-slice_fusion), channel_id=1, source_target_pairs={{0,4},{4,0},{1,5},{5,1},{2,6},{6,2},{3,7},{7,3},{8,12},{12,8},{9,1... | collective-permute-start | bytes 6291464 | tf_op jit(solution)/shard_map/ppermute | solution.py:441
  105.6 12.8 %all-to-all-start = ((bf16[32,2,768]{2,1,0:T(2,128)(2,1)}), bf16[32,2,768]{2,1,0:T(2,128)(2,1)S(1)}, u32[]{:S(2)}, u32[]{:S(2)}) async-start(bf16[32,2,768]{2,1,0:T(2,128)(2,1)} %reshape.483), calls=%async_computation | async-start | bytes 196608 | tf_op jit(solution)/shard_map/all_to_all | solution.py:458
  133.5 11.5 %all-to-all-start.1 = ((bf16[32,2,768]{2,1,0:T(2,128)(2,1)}), bf16[32,2,768]{2,1,0:T(2,128)(2,1)S(1)}, u32[]{:S(2)}, u32[]{:S(2)}) async-start(bf16[32,2,768]{2,1,0:T(2,128)(2,1)} %reshape.485), calls=%async_computation.1 | async-start | bytes 196608 | tf_op jit(solution)/shard_map/all_to_all | solution.py:464
  137.4 53.0 %all-gather.10.cloned.1.call-start = ((), (), s32[]{:S(2)}) async-start(), calls=%async_computation.4 | async-start | bytes 2785280 | tf_op jit(solution)/shard_map/all_gather | solution.py:470
  165.3 14.7 %collective-permute-start.3 = (bf16[64,4096]{1,0:T(8,128)(2,1)}, bf16[64,4096]{1,0:T(8,128)(2,1)S(1)}, u32[]{:S(2)}, u32[]{:S(2)}) collective-permute-start(bf16[64,4096]{1,0:T(8,128)(2,1)} %get-tuple-element.73), channel_id=1, source_target_pairs={{0,32},{32,64},{64,96},{96,0},{1,33},{33,65},{65,97},{97,1},{2,34}... | collective-permute-start | bytes 1572872 | tf_op jit(solution)/shard_map/ppermute | solution.py:353
  165.7 14.3 %collective-permute-start.4 = (bf16[64,4096]{1,0:T(8,128)(2,1)}, bf16[64,4096]{1,0:T(8,128)(2,1)S(1)}, u32[]{:S(2)}, u32[]{:S(2)}) collective-permute-start(bf16[64,4096]{1,0:T(8,128)(2,1)} %get-tuple-element.74), channel_id=1, source_target_pairs={{0,96},{32,0},{64,32},{96,64},{1,97},{33,1},{65,33},{97,65},{2,98}... | collective-permute-start | bytes 1572872 | tf_op jit(solution)/shard_map/ppermute | solution.py:353
  168.1 14.0 %collective-permute-start.5 = (bf16[64,4096]{1,0:T(8,128)(2,1)}, bf16[64,4096]{1,0:T(8,128)(2,1)S(1)}, u32[]{:S(2)}, u32[]{:S(2)}) collective-permute-start(bf16[64,4096]{1,0:T(8,128)(2,1)} %get-tuple-element.75), channel_id=1, source_target_pairs={{0,8},{8,16},{16,24},{24,0},{1,9},{9,17},{17,25},{25,1},{2,10},{10... | collective-permute-start | bytes 1572872 | tf_op jit(solution)/shard_map/ppermute | solution.py:353
  168.4 13.7 %collective-permute-start.6 = (bf16[64,4096]{1,0:T(8,128)(2,1)}, bf16[64,4096]{1,0:T(8,128)(2,1)S(1)}, u32[]{:S(2)}, u32[]{:S(2)}) collective-permute-start(bf16[64,4096]{1,0:T(8,128)(2,1)} %get-tuple-element.76), channel_id=1, source_target_pairs={{0,24},{8,0},{16,8},{24,16},{1,25},{9,1},{17,9},{25,17},{2,26},{10... | collective-permute-start | bytes 1572872 | tf_op jit(solution)/shard_map/ppermute | solution.py:353
  183.6 23.1 %collective-permute-start.10 = (bf16[128,4096]{1,0:T(8,128)(2,1)S(1)}, bf16[128,4096]{1,0:T(8,128)(2,1)}, u32[]{:S(2)}, u32[]{:S(2)}) collective-permute-start(bf16[128,4096]{1,0:T(8,128)(2,1)S(1)} %pad_maximum_fusion.4), channel_id=1, source_target_pairs={{0,24},{8,0},{16,8},{24,16},{1,25},{9,1},{17,9},{25,17},{2,26},{10... | collective-permute-start | bytes 3145736 | tf_op jit(solution)/shard_map/ppermute | solution.py:365
  186.1 23.7 %collective-permute-start.9 = (bf16[128,4096]{1,0:T(8,128)(2,1)S(1)}, bf16[128,4096]{1,0:T(8,128)(2,1)}, u32[]{:S(2)}, u32[]{:S(2)}) collective-permute-start(bf16[128,4096]{1,0:T(8,128)(2,1)S(1)} %pad_maximum_fusion.3), channel_id=1, source_target_pairs={{0,8},{8,16},{16,24},{24,0},{1,9},{9,17},{17,25},{25,1},{2,10},{10... | collective-permute-start | bytes 3145736 | tf_op jit(solution)/shard_map/ppermute | solution.py:365
  187.8 22.5 %collective-permute-start.8 = (bf16[128,4096]{1,0:T(8,128)(2,1)S(1)}, bf16[128,4096]{1,0:T(8,128)(2,1)}, u32[]{:S(2)}, u32[]{:S(2)}) collective-permute-start(bf16[128,4096]{1,0:T(8,128)(2,1)S(1)} %pad_maximum_fusion.2), channel_id=1, source_target_pairs={{0,96},{32,0},{64,32},{96,64},{1,97},{33,1},{65,33},{97,65},{2,98}... | collective-permute-start | bytes 3145736 | tf_op jit(solution)/shard_map/ppermute | solution.py:365
  189.2 23.9 %collective-permute-start.7 = (bf16[128,4096]{1,0:T(8,128)(2,1)}, bf16[128,4096]{1,0:T(8,128)(2,1)}, u32[]{:S(2)}, u32[]{:S(2)}) collective-permute-start(bf16[128,4096]{1,0:T(8,128)(2,1)} %pad_maximum_fusion.1), channel_id=1, source_target_pairs={{0,32},{32,64},{64,96},{96,0},{1,33},{33,65},{65,97},{97,1},{2,34}... | collective-permute-start | bytes 3145736 | tf_op jit(solution)/shard_map/ppermute | solution.py:365
  215.5 8.1 %collective-permute-start.13 = (bf16[16,4096]{1,0:T(8,128)(2,1)S(1)}, bf16[16,4096]{1,0:T(8,128)(2,1)S(1)}, u32[]{:S(2)}, u32[]{:S(2)}) collective-permute-start(bf16[16,4096]{1,0:T(8,128)(2,1)S(1)} %get-tuple-element.121), channel_id=1, source_target_pairs={{0,32},{32,64},{64,96},{96,0},{1,33},{33,65},{65,97},{97,1},{2,34}... | collective-permute-start | bytes 393224 | tf_op jit(solution)/shard_map/ppermute | solution.py:353
  215.6 8.1 %collective-permute-start.14 = (bf16[16,4096]{1,0:T(8,128)(2,1)S(1)}, bf16[16,4096]{1,0:T(8,128)(2,1)S(1)}, u32[]{:S(2)}, u32[]{:S(2)}) collective-permute-start(bf16[16,4096]{1,0:T(8,128)(2,1)S(1)} %get-tuple-element.120), channel_id=1, source_target_pairs={{0,96},{32,0},{64,32},{96,64},{1,97},{33,1},{65,33},{97,65},{2,98}... | collective-permute-start | bytes 393224 | tf_op jit(solution)/shard_map/ppermute | solution.py:353
  220.6 5.4 %collective-permute-start.11 = (bf16[16,4096]{1,0:T(8,128)(2,1)S(1)}, bf16[16,4096]{1,0:T(8,128)(2,1)S(1)}, u32[]{:S(2)}, u32[]{:S(2)}) collective-permute-start(bf16[16,4096]{1,0:T(8,128)(2,1)S(1)} %get-tuple-element.127), channel_id=1, source_target_pairs={{0,8},{8,16},{16,24},{24,0},{1,9},{9,17},{17,25},{25,1},{2,10},{10... | collective-permute-start | bytes 393224 | tf_op jit(solution)/shard_map/ppermute | solution.py:353
  220.9 5.0 %collective-permute-start.12 = (bf16[16,4096]{1,0:T(8,128)(2,1)S(1)}, bf16[16,4096]{1,0:T(8,128)(2,1)S(1)}, u32[]{:S(2)}, u32[]{:S(2)}) collective-permute-start(bf16[16,4096]{1,0:T(8,128)(2,1)S(1)} %get-tuple-element.126), channel_id=1, source_target_pairs={{0,24},{8,0},{16,8},{24,16},{1,25},{9,1},{17,9},{25,17},{2,26},{10... | collective-permute-start | bytes 393224 | tf_op jit(solution)/shard_map/ppermute | solution.py:353
  226.1 5.3 %collective-permute-start.18 = (bf16[32,4096]{1,0:T(8,128)(2,1)S(1)}, bf16[32,4096]{1,0:T(8,128)(2,1)S(1)}, u32[]{:S(2)}, u32[]{:S(2)}) collective-permute-start(bf16[32,4096]{1,0:T(8,128)(2,1)S(1)} %pad_maximum_fusion.9), channel_id=1, source_target_pairs={{0,96},{32,0},{64,32},{96,64},{1,97},{33,1},{65,33},{97,65},{2,98}... | collective-permute-start | bytes 786440 | tf_op jit(solution)/shard_map/ppermute | solution.py:365
  226.5 6.6 %collective-permute-start.17 = (bf16[32,4096]{1,0:T(8,128)(2,1)S(1)}, bf16[32,4096]{1,0:T(8,128)(2,1)}, u32[]{:S(2)}, u32[]{:S(2)}) collective-permute-start(bf16[32,4096]{1,0:T(8,128)(2,1)S(1)} %pad_maximum_fusion.8), channel_id=1, source_target_pairs={{0,32},{32,64},{64,96},{96,0},{1,33},{33,65},{65,97},{97,1},{2,34}... | collective-permute-start | bytes 786440 | tf_op jit(solution)/shard_map/ppermute | solution.py:365
  227.8 6.1 %collective-permute-start.16 = (bf16[32,4096]{1,0:T(8,128)(2,1)S(1)}, bf16[32,4096]{1,0:T(8,128)(2,1)}, u32[]{:S(2)}, u32[]{:S(2)}) collective-permute-start(bf16[32,4096]{1,0:T(8,128)(2,1)S(1)} %pad_maximum_fusion.7), channel_id=1, source_target_pairs={{0,24},{8,0},{16,8},{24,16},{1,25},{9,1},{17,9},{25,17},{2,26},{10... | collective-permute-start | bytes 786440 | tf_op jit(solution)/shard_map/ppermute | solution.py:365
  230.5 6.9 %collective-permute-start.15 = (bf16[32,4096]{1,0:T(8,128)(2,1)S(1)}, bf16[32,4096]{1,0:T(8,128)(2,1)}, u32[]{:S(2)}, u32[]{:S(2)}) collective-permute-start(bf16[32,4096]{1,0:T(8,128)(2,1)S(1)} %pad_maximum_fusion.6), channel_id=1, source_target_pairs={{0,8},{8,16},{16,24},{24,0},{1,9},{9,17},{17,25},{25,1},{2,10},{10... | collective-permute-start | bytes 786440 | tf_op jit(solution)/shard_map/ppermute | solution.py:365
  239.7 8.2 %collective-permute-start.19 = (bf16[2,16,4096]{2,1,0:T(8,128)(2,1)S(1)}, bf16[2,16,4096]{2,1,0:T(8,128)(2,1)S(1)}, u32[]{:S(2)}, u32[]{:S(2)}) collective-permute-start(bf16[2,16,4096]{2,1,0:T(8,128)(2,1)S(1)} %get-tuple-element.133), channel_id=1, source_target_pairs={{0,4},{4,0},{1,5},{5,1},{2,6},{6,2},{3,7},{7,3},{8,12},{12,8},{9,1... | collective-permute-start | bytes 786440 | tf_op jit(solution)/shard_map/ppermute | solution.py:500
  (10 other events, 116.7 us)
Sparse Core Ops, SparseCore 0:
  10.8 76.2 all-gather.5
  103.1 47.3 all-gather.7
  152.1 32.1 all-gather.9
